TPU v7x, 32 devices: a whole 2x2x4 slice. The times are simulated.
32 devices in a mesh: sect: 4 (over z), sec: 8 (over y, x, core).
Axes of the slice: x: 2, y: 2, z: 4, core: 2. Of those that a mesh axis runs over, the one named last changes fastest.
Arguments:
- psi_start: float32 [4, 2048, 32, 400], P('sect', 'sec'), may hold values from -6 to 6
- left_blocks: bfloat16 [4, 3, 1, 2048, 256], P('sect', None, None, 'sec'), may hold values from -0.375 to 0.375
- site_ops: bfloat16 [4, 3, 400, 400], P('sect'), may hold values from -0.3125 to 0.3125
- site_tensors: float32 [4, 256, 20, 32], P('sect', 'sec'), may hold values from -0.5 to 0.5
- env_ops: float32 [4, 3, 20, 20], P('sect'), may hold values from -1.25 to 1.25
- boundary: float32 [3, 256, 32], P(None, 'sec'), may hold values from -6 to 6
- precond: float32 [4, 2048, 32, 400], P('sect', 'sec'), may hold values from 8 to 64
Outputs:
- psi_opt: float32 [4, 2048, 32, 400], P('sect', 'sec')
- energies: float32 [4], P('sect')
All inputs are finite; a program needn't handle non-finite values.
Results may differ from a plain program's by a relative error of at most 0.015.
Values may be sent and summed in bfloat16 or wider, within the bound.
A program may use at most 192 MiB of HBM per device.

v0:
```python
import jax
import jax.numpy as jnp
from jax import lax
from jax.sharding import PartitionSpec as P

ITERS = 4


def from_behind(shard, axis, by):
    count = lax.axis_size(axis)
    pairs = [(i, i + by) for i in range(count) if 0 <= i + by < count]
    return lax.ppermute(shard, axis, pairs)


def with_halo(block, sides, width):
    for axis, dim in sides:
        count = lax.axis_size(axis)
        forward = [(i, i + 1) for i in range(count - 1)]
        backward = [(target, source) for source, target in forward]
        low = lax.ppermute(
            lax.slice_in_dim(block, block.shape[dim] - width, None, axis=dim), axis, forward
        )
        high = lax.ppermute(lax.slice_in_dim(block, 0, width, axis=dim), axis, backward)
        block = jnp.concatenate([low, block, high], axis=dim)
    return block


def apply_columns(factors, operators, environ):
    mixed = jnp.einsum("kmbs,kts->kmbt", factors, operators, preferred_element_type=jnp.float32)
    mixed = mixed.astype(jnp.bfloat16)
    return jnp.einsum("kcb,kmbt->mct", environ, mixed, preferred_element_type=jnp.float32)


def couple_rows(blocks, vector_rows):
    product = jnp.einsum("krj,jbs->krbs", blocks, vector_rows, preferred_element_type=jnp.float32)
    return product.astype(jnp.bfloat16)


def advance(tensors, operators, environ):
    highest = lax.Precision.HIGHEST
    first = jnp.einsum("cpx,kxy->kcpy", tensors, environ, precision=highest)
    second = jnp.einsum("kcpy,kpz->kczy", first, operators, precision=highest)
    return jnp.einsum("kczy,bzy->kcb", second, tensors, precision=highest)


def on_device(psi_start, left_blocks, site_ops, site_tensors, env_ops, boundary, precond):
    tensors_here = site_tensors[0]
    operators_here = env_ops[0]
    position_sect = lax.axis_index("sect")
    final_sect = lax.axis_size("sect") - 1
    current = advance(tensors_here, operators_here, boundary)
    for step in range(lax.axis_size("sect") - 1):
        received = from_behind(current, "sect", -1)
        current = jnp.where(
            position_sect == final_sect, current, advance(tensors_here, operators_here, received)
        )
    vector = psi_start[0]
    row_count, bond_size, pair_count = vector.shape
    environ = current.astype(jnp.bfloat16)
    operators = site_ops[0]
    couplings = left_blocks[0]
    inverse = 1.0 / precond[0]
    cell_count = row_count * bond_size * pair_count * lax.axis_size("sec")
    ritz_value = jnp.float32(0.0)
    for iteration in range(ITERS):
        lowered = vector.astype(jnp.bfloat16)
        padded = with_halo(lowered, (("sec", 0),), row_count)
        pieces = []
        for position in range(3):
            nearby = padded[position * row_count : (position + 1) * row_count]
            pieces.append(couple_rows(couplings[position], nearby))
        image = apply_columns(jnp.concatenate(pieces, axis=0), operators, environ)
        intersection, norm_sq = lax.psum((jnp.sum(vector * image), jnp.sum(vector * vector)), "sec")
        ritz_value = intersection / norm_sq
        updated = vector - (image - ritz_value * vector) * inverse
        length = lax.psum(jnp.sum(updated * updated), "sec")
        vector = updated * lax.rsqrt(length / cell_count + 1e-06)
    return (vector[None], jnp.reshape(ritz_value, (1,)))


def solution(mesh):
    placed = (
        P("sect", "sec", None, None),
        P("sect", None, None, "sec", None),
        P("sect", None, None, None),
        P("sect", "sec", None, None),
        P("sect", None, None, None),
        P(None, "sec", None),
        P("sect", "sec", None, None),
    )
    return jax.shard_map(
        on_device,
        mesh=mesh,
        in_specs=placed,
        out_specs=(P("sect", "sec", None, None), P("sect")),
        check_vma=False,
    )
```

profile of v0, /device:TPU:0, one launch (start us, length us, event | category | flops | bytes accessed | tf_op | source)
XLA Modules:
  0.0 1037.5 jit_solution(9862184483839860260)
XLA Ops:
  0.7 8.3 bitcast_convert_fusion
  10.2 5.7 collective-permute-start
  16.0 2.7 fusion.91
  18.7 1.9 copy.16
  20.6 7.2 fusion.66
  27.8 1.6 copy.18
  31.8 5.5 collective-permute-done.2
  37.3 2.7 fusion.88
  40.1 1.9 copy.21
  41.9 7.2 fusion.64
  49.2 1.6 copy.22
  53.0 4.7 collective-permute-done.3
  57.7 2.7 fusion.85
  60.4 1.9 copy.25
  62.3 7.2 fusion.62
  69.5 1.6 copy.26
  72.1 1.5 collective-permute-start.4
  73.6 9.4 fusion.46
  83.0 2.7 fusion.82
  85.7 1.9 copy.29
  87.6 7.2 fusion.60
  94.8 1.6 copy.30
  97.3 7.5 fusion.50
  104.9 7.5 fusion.49
  112.4 20.1 %fusion.4 = bf16[3,256,32,400]{1,3,2,0:T(8,128)(2,1)} fusion(bf16[1,256,32,400]{1,3,2,0:T(8,128)(2,1)} %fusion.50, bf16[1,256,32,400]{1,3,2,0:T(8,128)(2,1)} %fusion.46, bf16[1,256,32,400]{1,3,2,0:T(8,128)(2,1)} %fusion.49, bf16[1,3,400,400]{3,2,1,0:T(8,128)(2,1)S(1)} %copy-done), kind=kOutput, calls=%fused_computation.8 | convolution fusion | flops 7923302400 | bytes 40281600 | tf_op jit(solution)/shard_map/kmbs,kts->kmbt/dot_general | solution.py:29
  132.5 13.1 %fusion.43 = f32[256,400,32]{0,2,1:T(8,128)S(1)} fusion(bf16[3,32,32,1]{2,1,0,3:T(8,128)(2,1)S(1)} %fusion.76, bf16[3,256,32,400]{1,3,2,0:T(8,128)(2,1)} %fusion.4), kind=kOutput, calls=%fused_computation.70 | convolution fusion | flops 629145600 | bytes 32774144 | tf_op jit(solution)/shard_map/kcb,kmbt->mct/dot_general | solution.py:31
  145.6 14.2 %fusion.39 = (f32[]{:T(128)}, f32[]{:T(128)}) fusion(f32[1,256,32,400]{1,3,2,0:T(8,128)} %param.7, f32[256,400,32]{0,2,1:T(8,128)S(1)} %fusion.43), kind=kLoop, calls=%fused_computation.55 | loop fusion | flops 13107198 | bytes 26214408 | tf_op jit(solution)/shard_map/reduce_sum | solution.py:73
  159.8 68.3 %all-reduce.3 = (f32[]{:T(128)}, f32[]{:T(128)}) all-reduce(f32[]{:T(128)} %get-tuple-element.9, f32[]{:T(128)} %get-tuple-element.8), channel_id=1, replica_groups=mesh['sect'=4,'sec'=8] {'sec'}, use_global_device_ids=true, to_apply=%region_1.2 | all-reduce | flops 2 | bytes 16 | tf_op jit(solution)/shard_map/psum | solution.py:73
  229.4 18.8 %multiply_reduce_fusion.6 = (f32[]{:T(128)}, f32[256,32,400]{0,2,1:T(8,128)}) fusion(f32[1,256,32,400]{1,3,2,0:T(8,128)} %param.13, f32[]{:T(128)S(6)} %div.33, f32[256,400,32]{0,2,1:T(8,128)} %copy-done.4, f32[1,256,32,400]{1,3,2,0:T(8,128)} %param.7), kind=kLoop, calls=%fused_computation.63 | loop fusion | flops 22937600 | bytes 52428808 | tf_op jit(solution)/shard_map/reduce_sum | solution.py:76
  248.2 12.4 %psum.86 = f32[]{:T(128)} all-reduce(f32[]{:T(128)} %get-tuple-element.24), channel_id=1, replica_groups=mesh['sect'=4,'sec'=8] {'sec'}, use_global_device_ids=true, to_apply=%region_5.6 | all-reduce | flops 1 | bytes 8 | tf_op jit(solution)/shard_map/psum | solution.py:76
  261.3 8.6 multiply_convert_fusion.2
  271.2 3.5 collective-permute-start.5
  274.7 7.4 fusion.52
  282.6 4.7 fusion.53
  287.2 4.7 fusion.51
  291.9 19.9 %fusion.10 = bf16[3,256,32,400]{1,3,2,0:T(8,128)(2,1)} fusion(bf16[1,256,32,400]{1,3,2,0:T(8,128)(2,1)} %fusion.53, bf16[1,256,32,400]{1,3,2,0:T(8,128)(2,1)} %fusion.52, bf16[1,256,32,400]{1,3,2,0:T(8,128)(2,1)} %fusion.51, bf16[1,3,400,400]{3,2,1,0:T(8,128)(2,1)S(1)} %copy-done), kind=kOutput, calls=%fused_computation.14 | convolution fusion | flops 7923302400 | bytes 40281600 | tf_op jit(solution)/shard_map/kmbs,kts->kmbt/dot_general | solution.py:29
  311.8 13.1 %fusion.42 = f32[256,400,32]{0,2,1:T(8,128)S(1)} fusion(bf16[3,32,32,1]{2,1,0,3:T(8,128)(2,1)S(1)} %fusion.76, bf16[3,256,32,400]{1,3,2,0:T(8,128)(2,1)} %fusion.10), kind=kOutput, calls=%fused_computation.69 | convolution fusion | flops 629145600 | bytes 32774144 | tf_op jit(solution)/shard_map/kcb,kmbt->mct/dot_general | solution.py:31
  324.9 14.2 %multiply_reduce_fusion.5 = (f32[]{:T(128)}, f32[]{:T(128)}) fusion(f32[256,32,400]{0,2,1:T(8,128)} %get-tuple-element.25, f32[]{:T(128)S(6)} %rsqrt.12, f32[256,400,32]{0,2,1:T(8,128)S(1)} %fusion.42), kind=kLoop, calls=%fused_computation.62 | loop fusion | flops 16383998 | bytes 26214412 | tf_op jit(solution)/shard_map/reduce_sum | solution.py:73
  339.1 143.7 %all-reduce.2 = (f32[]{:T(128)}, f32[]{:T(128)}) all-reduce(f32[]{:T(128)} %get-tuple-element.7, f32[]{:T(128)} %get-tuple-element.6), channel_id=1, replica_groups=mesh['sect'=4,'sec'=8] {'sec'}, use_global_device_ids=true, to_apply=%region_7.8 | all-reduce | flops 2 | bytes 16 | tf_op jit(solution)/shard_map/psum | solution.py:73
  484.1 18.8 %multiply_reduce_fusion.4 = (f32[]{:T(128)}, f32[256,32,400]{0,2,1:T(8,128)}) fusion(f32[1,256,32,400]{1,3,2,0:T(8,128)} %param.13, f32[]{:T(128)S(6)} %div.38, f32[256,400,32]{0,2,1:T(8,128)} %copy-done.2, f32[256,32,400]{0,2,1:T(8,128)} %get-tuple-element.25, f32[]{:T(128)S(6)} %rsqrt.12), kind=kLoop, calls=%fused_computation.61 | loop fusion | flops 26214400 | bytes 52428812 | tf_op jit(solution)/shard_map/reduce_sum | solution.py:76
  502.9 12.4 %psum.89 = f32[]{:T(128)} all-reduce(f32[]{:T(128)} %get-tuple-element.22), channel_id=1, replica_groups=mesh['sect'=4,'sec'=8] {'sec'}, use_global_device_ids=true, to_apply=%region_11.12 | all-reduce | flops 1 | bytes 8 | tf_op jit(solution)/shard_map/psum | solution.py:76
  516.0 8.6 multiply_convert_fusion.1
  525.9 3.5 collective-permute-start.7
  529.4 7.5 fusion.55
  537.3 4.7 fusion.56
  541.9 4.7 fusion.54
  546.6 19.8 %fusion.16 = bf16[3,256,32,400]{1,3,2,0:T(8,128)(2,1)} fusion(bf16[1,256,32,400]{1,3,2,0:T(8,128)(2,1)} %fusion.56, bf16[1,256,32,400]{1,3,2,0:T(8,128)(2,1)} %fusion.55, bf16[1,256,32,400]{1,3,2,0:T(8,128)(2,1)} %fusion.54, bf16[1,3,400,400]{3,2,1,0:T(8,128)(2,1)S(1)} %copy-done), kind=kOutput, calls=%fused_computation.20 | convolution fusion | flops 7923302400 | bytes 40281600 | tf_op jit(solution)/shard_map/kmbs,kts->kmbt/dot_general | solution.py:29
  566.5 13.1 %fusion.41 = f32[256,400,32]{0,2,1:T(8,128)S(1)} fusion(bf16[3,32,32,1]{2,1,0,3:T(8,128)(2,1)S(1)} %fusion.76, bf16[3,256,32,400]{1,3,2,0:T(8,128)(2,1)} %fusion.16), kind=kOutput, calls=%fused_computation.68 | convolution fusion | flops 629145600 | bytes 32774144 | tf_op jit(solution)/shard_map/kcb,kmbt->mct/dot_general | solution.py:31
  579.6 14.2 %multiply_reduce_fusion.3 = (f32[]{:T(128)}, f32[]{:T(128)}) fusion(f32[256,32,400]{0,2,1:T(8,128)} %get-tuple-element.23, f32[]{:T(128)S(6)} %rsqrt.13, f32[256,400,32]{0,2,1:T(8,128)S(1)} %fusion.41), kind=kLoop, calls=%fused_computation.60 | loop fusion | flops 16383998 | bytes 26214412 | tf_op jit(solution)/shard_map/reduce_sum | solution.py:73
  593.8 143.5 %all-reduce.1 = (f32[]{:T(128)}, f32[]{:T(128)}) all-reduce(f32[]{:T(128)} %get-tuple-element.5, f32[]{:T(128)} %get-tuple-element.4), channel_id=1, replica_groups=mesh['sect'=4,'sec'=8] {'sec'}, use_global_device_ids=true, to_apply=%region_13.14 | all-reduce | flops 2 | bytes 16 | tf_op jit(solution)/shard_map/psum | solution.py:73
  738.6 18.8 %multiply_reduce_fusion.2 = (f32[]{:T(128)}, f32[256,32,400]{0,2,1:T(8,128)}) fusion(f32[1,256,32,400]{1,3,2,0:T(8,128)} %param.13, f32[]{:T(128)S(6)} %div.40, f32[256,400,32]{0,2,1:T(8,128)} %copy-done.3, f32[256,32,400]{0,2,1:T(8,128)} %get-tuple-element.23, f32[]{:T(128)S(6)} %rsqrt.13), kind=kLoop, calls=%fused_computation.59 | loop fusion | flops 26214400 | bytes 52428812 | tf_op jit(solution)/shard_map/reduce_sum | solution.py:76
  757.4 12.4 %psum.92 = f32[]{:T(128)} all-reduce(f32[]{:T(128)} %get-tuple-element.20), channel_id=1, replica_groups=mesh['sect'=4,'sec'=8] {'sec'}, use_global_device_ids=true, to_apply=%region_17.18 | all-reduce | flops 1 | bytes 8 | tf_op jit(solution)/shard_map/psum | solution.py:76
  770.5 8.6 multiply_convert_fusion
  780.4 3.5 collective-permute-start.9
  783.9 7.4 fusion.58
  791.8 4.7 fusion.59
  796.4 4.7 fusion.57
  801.1 19.9 %fusion.22 = bf16[3,256,32,400]{1,3,2,0:T(8,128)(2,1)} fusion(bf16[1,256,32,400]{1,3,2,0:T(8,128)(2,1)} %fusion.59, bf16[1,256,32,400]{1,3,2,0:T(8,128)(2,1)} %fusion.58, bf16[1,256,32,400]{1,3,2,0:T(8,128)(2,1)} %fusion.57, bf16[1,3,400,400]{3,2,1,0:T(8,128)(2,1)S(1)} %copy-done), kind=kOutput, calls=%fused_computation.26 | convolution fusion | flops 7923302400 | bytes 40281600 | tf_op jit(solution)/shard_map/kmbs,kts->kmbt/dot_general | solution.py:29
  821.0 13.1 %fusion.40 = f32[256,400,32]{0,2,1:T(8,128)S(1)} fusion(bf16[3,32,32,1]{2,1,0,3:T(8,128)(2,1)S(1)} %fusion.76, bf16[3,256,32,400]{1,3,2,0:T(8,128)(2,1)} %fusion.22), kind=kOutput, calls=%fused_computation.67 | convolution fusion | flops 629145600 | bytes 32774144 | tf_op jit(solution)/shard_map/kcb,kmbt->mct/dot_general | solution.py:31
  834.1 14.2 %multiply_reduce_fusion.1 = (f32[]{:T(128)}, f32[]{:T(128)}) fusion(f32[256,32,400]{0,2,1:T(8,128)} %get-tuple-element.21, f32[]{:T(128)S(6)} %rsqrt.14, f32[256,400,32]{0,2,1:T(8,128)S(1)} %fusion.40), kind=kLoop, calls=%fused_computation.58 | loop fusion | flops 16383998 | bytes 26214412 | tf_op jit(solution)/shard_map/reduce_sum | solution.py:73
  848.4 143.6 %all-reduce = (f32[]{:T(128)}, f32[]{:T(128)}) all-reduce(f32[]{:T(128)} %get-tuple-element.3, f32[]{:T(128)} %get-tuple-element.2), channel_id=1, replica_groups=mesh['sect'=4,'sec'=8] {'sec'}, use_global_device_ids=true, to_apply=%region_19.20 | all-reduce | flops 2 | bytes 16 | tf_op jit(solution)/shard_map/psum | solution.py:73
  993.2 18.9 %multiply_reduce_fusion = (f32[]{:T(128)}, f32[256,32,400]{0,2,1:T(8,128)}) fusion(f32[1,256,32,400]{1,3,2,0:T(8,128)} %param.13, f32[]{:T(128)} %div.42, f32[256,400,32]{0,2,1:T(8,128)} %copy-done.1, f32[256,32,400]{0,2,1:T(8,128)} %get-tuple-element.21, f32[]{:T(128)S(6)} %rsqrt.14), kind=kLoop, calls=%fused_computation.57 | loop fusion | flops 26214400 | bytes 52428812 | tf_op jit(solution)/shard_map/reduce_sum | solution.py:76
  1012.1 12.4 %psum.95 = f32[]{:T(128)} all-reduce(f32[]{:T(128)} %get-tuple-element.18), channel_id=1, replica_groups=mesh['sect'=4,'sec'=8] {'sec'}, use_global_device_ids=true, to_apply=%region_23.24 | all-reduce | flops 1 | bytes 8 | tf_op jit(solution)/shard_map/psum | solution.py:76
  1025.2 10.6 %multiply_bitcast_fusion = f32[1,256,32,400]{1,3,2,0:T(8,128)} fusion(f32[256,32,400]{0,2,1:T(8,128)} %get-tuple-element.19, f32[]{:T(128)S(6)} %rsqrt.15), kind=kLoop, calls=%fused_computation.56 | loop fusion | flops 3276800 | bytes 26214404 | tf_op jit(solution)/shard_map/broadcast_in_dim | solution.py:78
  (49 shorter events, 12.8 us)
Async XLA Ops:
  0.6 111.8 %copy-start = (bf16[1,3,400,400]{3,2,1,0:T(8,128)(2,1)S(1)}, bf16[1,3,400,400]{3,2,1,0:T(8,128)(2,1)}, u32[]{:S(2)}) copy-start(bf16[1,3,400,400]{3,2,1,0:T(8,128)(2,1)} %param.9) | copy-start | bytes 2880004
  0.6 15.3 %copy-start.5 = (f32[1,32,20,32]{3,1,2,0:T(8,128)S(1)}, f32[1,32,20,32]{3,1,2,0:T(8,128)}, u32[]{:S(2)}) copy-start(f32[1,32,20,32]{3,1,2,0:T(8,128)} %param.10) | copy-start | bytes 245764
  0.7 15.3 %copy-start.14 = (f32[3,32,32]{2,1,0:T(8,128)S(1)}, f32[3,32,32]{2,1,0:T(8,128)}, u32[]{:S(2)}) copy-start(f32[3,32,32]{2,1,0:T(8,128)} %param.12) | copy-start | bytes 36868
  0.7 19.9 %copy-start.10 = (f32[1,3,20,20]{3,0,2,1:T(1,128)S(1)}, f32[1,3,20,20]{3,0,2,1:T(1,128)}, u32[]{:S(2)}) copy-start(f32[1,3,20,20]{3,0,2,1:T(1,128)} %param.11) | copy-start | bytes 14404
  8.9 88.4 %collective-permute-start.1 = (bf16[256,32,400]{0,2,1:T(8,128)(2,1)}, bf16[256,32,400]{0,2,1:T(8,128)(2,1)}, u32[]{:S(2)}, u32[]{:S(2)}) collective-permute-start(bf16[256,32,400]{0,2,1:T(8,128)(2,1)} %bitcast_convert_fusion), channel_id=1, source_target_pairs={{1,0},{2,1},{3,2},{4,3},{5,4},{6,5},{7,6},{9,8},{10,9},{11,10},{12... | collective-permute-start | bytes 19660808 | tf_op jit(solution)/shard_map/ppermute | solution.py:23
  10.2 94.7 %collective-permute-start = (bf16[256,32,400]{0,2,1:T(8,128)(2,1)}, bf16[256,32,400]{0,2,1:T(8,128)(2,1)}, u32[]{:S(2)}, u32[]{:S(2)}) collective-permute-start(bf16[256,32,400]{0,2,1:T(8,128)(2,1)} %bitcast_convert_fusion), channel_id=1, source_target_pairs={{0,1},{1,2},{2,3},{3,4},{4,5},{5,6},{6,7},{8,9},{9,10},{10,11},{11... | collective-permute-start | bytes 19660808 | tf_op jit(solution)/shard_map/ppermute | solution.py:20
  20.6 53.0 %copy-start.6 = (bf16[1,3,1,256,256]{4,3,2,1,0:T(8,128)(2,1)S(1)}, bf16[1,3,1,256,256]{4,3,2,1,0:T(8,128)(2,1)}, u32[]{:S(2)}) copy-start(bf16[1,3,1,256,256]{4,3,2,1,0:T(8,128)(2,1)} %param.8) | copy-start | bytes 1179652
  30.3 7.0 copy-start.13
  30.3 7.0 collective-permute-start.2
  51.7 6.0 copy-start.12
  51.7 6.0 collective-permute-start.3
  72.0 10.9 %copy-start.11 = (f32[3,32,32]{2,1,0:T(8,128)}, f32[3,32,32]{2,1,0:T(8,128)S(1)}, u32[]{:S(2)}) copy-start(f32[3,32,32]{2,1,0:T(8,128)S(1)} %fusion.73) | copy-start | bytes 36868
  72.1 10.9 %collective-permute-start.4 = (f32[3,32,32]{2,1,0:T(8,128)S(1)}, f32[3,32,32]{2,1,0:T(8,128)S(1)}, u32[]{:S(2)}, u32[]{:S(2)}) collective-permute-start(f32[3,32,32]{2,1,0:T(8,128)S(1)} %fusion.73), channel_id=1, source_target_pairs={{8,0},{16,8},{24,16},{9,1},{17,9},{25,17},{10,2},{18,10},{26,18},{... | collective-permute-start | bytes 36872 | tf_op jit(solution)/shard_map/ppermute | solution.py:12
  145.6 14.2 %copy-start.4 = (f32[256,400,32]{0,2,1:T(8,128)}, f32[256,400,32]{0,2,1:T(8,128)S(1)}, u32[]{:S(2)}) copy-start(f32[256,400,32]{0,2,1:T(8,128)S(1)} %fusion.43) | copy-start | bytes 39321604
  248.2 26.5 %copy-start.7 = (bf16[1,3,1,256,256]{4,3,2,1,0:T(8,128)(2,1)S(1)}, bf16[1,3,1,256,256]{4,3,2,1,0:T(8,128)(2,1)}, u32[]{:S(2)}) copy-start(bf16[1,3,1,256,256]{4,3,2,1,0:T(8,128)(2,1)} %param.8) | copy-start | bytes 1179652
  269.9 12.6 %collective-permute-start.6 = (bf16[256,32,400]{0,2,1:T(8,128)(2,1)}, bf16[256,32,400]{0,2,1:T(8,128)(2,1)S(1)}, u32[]{:S(2)}, u32[]{:S(2)}) collective-permute-start(bf16[256,32,400]{0,2,1:T(8,128)(2,1)} %multiply_convert_fusion.2), channel_id=1, source_target_pairs={{1,0},{2,1},{3,2},{4,3},{5,4},{6,5},{7,6},{9,8},{10,9},{11,10},{12... | collective-permute-start | bytes 19660808 | tf_op jit(solution)/shard_map/ppermute | solution.py:23
  271.2 16.0 %collective-permute-start.5 = (bf16[256,32,400]{0,2,1:T(8,128)(2,1)}, bf16[256,32,400]{0,2,1:T(8,128)(2,1)S(1)}, u32[]{:S(2)}, u32[]{:S(2)}) collective-permute-start(bf16[256,32,400]{0,2,1:T(8,128)(2,1)} %multiply_convert_fusion.2), channel_id=1, source_target_pairs={{0,1},{1,2},{2,3},{3,4},{4,5},{5,6},{6,7},{8,9},{9,10},{10,11},{11... | collective-permute-start | bytes 19660808 | tf_op jit(solution)/shard_map/ppermute | solution.py:20
  324.9 14.2 %copy-start.2 = (f32[256,400,32]{0,2,1:T(8,128)}, f32[256,400,32]{0,2,1:T(8,128)S(1)}, u32[]{:S(2)}) copy-start(f32[256,400,32]{0,2,1:T(8,128)S(1)} %fusion.42) | copy-start | bytes 39321604
  502.9 26.5 %copy-start.8 = (bf16[1,3,1,256,256]{4,3,2,1,0:T(8,128)(2,1)S(1)}, bf16[1,3,1,256,256]{4,3,2,1,0:T(8,128)(2,1)}, u32[]{:S(2)}) copy-start(bf16[1,3,1,256,256]{4,3,2,1,0:T(8,128)(2,1)} %param.8) | copy-start | bytes 1179652
  524.7 12.6 %collective-permute-start.8 = (bf16[256,32,400]{0,2,1:T(8,128)(2,1)}, bf16[256,32,400]{0,2,1:T(8,128)(2,1)S(1)}, u32[]{:S(2)}, u32[]{:S(2)}) collective-permute-start(bf16[256,32,400]{0,2,1:T(8,128)(2,1)} %multiply_convert_fusion.1), channel_id=1, source_target_pairs={{1,0},{2,1},{3,2},{4,3},{5,4},{6,5},{7,6},{9,8},{10,9},{11,10},{12... | collective-permute-start | bytes 19660808 | tf_op jit(solution)/shard_map/ppermute | solution.py:23
  525.9 16.0 %collective-permute-start.7 = (bf16[256,32,400]{0,2,1:T(8,128)(2,1)}, bf16[256,32,400]{0,2,1:T(8,128)(2,1)S(1)}, u32[]{:S(2)}, u32[]{:S(2)}) collective-permute-start(bf16[256,32,400]{0,2,1:T(8,128)(2,1)} %multiply_convert_fusion.1), channel_id=1, source_target_pairs={{0,1},{1,2},{2,3},{3,4},{4,5},{5,6},{6,7},{8,9},{9,10},{10,11},{11... | collective-permute-start | bytes 19660808 | tf_op jit(solution)/shard_map/ppermute | solution.py:20
  579.6 14.2 %copy-start.3 = (f32[256,400,32]{0,2,1:T(8,128)}, f32[256,400,32]{0,2,1:T(8,128)S(1)}, u32[]{:S(2)}) copy-start(f32[256,400,32]{0,2,1:T(8,128)S(1)} %fusion.41) | copy-start | bytes 39321604
  757.4 26.5 %copy-start.9 = (bf16[1,3,1,256,256]{4,3,2,1,0:T(8,128)(2,1)S(1)}, bf16[1,3,1,256,256]{4,3,2,1,0:T(8,128)(2,1)}, u32[]{:S(2)}) copy-start(bf16[1,3,1,256,256]{4,3,2,1,0:T(8,128)(2,1)} %param.8) | copy-start | bytes 1179652
  779.1 12.6 %collective-permute-start.10 = (bf16[256,32,400]{0,2,1:T(8,128)(2,1)}, bf16[256,32,400]{0,2,1:T(8,128)(2,1)S(1)}, u32[]{:S(2)}, u32[]{:S(2)}) collective-permute-start(bf16[256,32,400]{0,2,1:T(8,128)(2,1)} %multiply_convert_fusion), channel_id=1, source_target_pairs={{1,0},{2,1},{3,2},{4,3},{5,4},{6,5},{7,6},{9,8},{10,9},{11,10},{12... | collective-permute-start | bytes 19660808 | tf_op jit(solution)/shard_map/ppermute | solution.py:23
  780.4 16.0 %collective-permute-start.9 = (bf16[256,32,400]{0,2,1:T(8,128)(2,1)}, bf16[256,32,400]{0,2,1:T(8,128)(2,1)S(1)}, u32[]{:S(2)}, u32[]{:S(2)}) collective-permute-start(bf16[256,32,400]{0,2,1:T(8,128)(2,1)} %multiply_convert_fusion), channel_id=1, source_target_pairs={{0,1},{1,2},{2,3},{3,4},{4,5},{5,6},{6,7},{8,9},{9,10},{10,11},{11... | collective-permute-start | bytes 19660808 | tf_op jit(solution)/shard_map/ppermute | solution.py:20
  834.1 14.2 %copy-start.1 = (f32[256,400,32]{0,2,1:T(8,128)}, f32[256,400,32]{0,2,1:T(8,128)S(1)}, u32[]{:S(2)}) copy-start(f32[256,400,32]{0,2,1:T(8,128)S(1)} %fusion.40) | copy-start | bytes 39321604
where the time goes:
time: 1050 us; the launch traced here: 1040 us
  blocking collectives  549 us (52%)
  matrix products  251 us (24%)
  other arithmetic  177 us (17%)
  starting transfers between devices  25.5 us (2%)
  local copies, waits for them, and re-layouts  13.8 us (1%)
  waiting for transfers between devices  11.4 us (1%)
    psum x4, blocking collectives, on_device(): lax.psum((jnp.sum(vector * image), jnp.sum(vector * vector)), 'sec')  499 us
    dot_general x4, matrix products, apply_columns(): jnp.einsum('kmbs,kts->kmbt', factors, operators, preferred_element_type=j...  79.6 us
    reduce_sum x4, other arithmetic, on_device(): length = lax.psum(jnp.sum(updated * updated), 'sec')  75.4 us
    dot_general x12, matrix products, couple_rows(): jnp.einsum('krj,jbs->krbs', blocks, vector_rows, preferred_element_type=j...  75 us
    reduce_sum x4, other arithmetic, on_device(): jnp.sum(vector * vector)  56.9 us
    dot_general x4, matrix products, apply_columns(): jnp.einsum('kcb,kmbt->mct', environ, mixed, preferred_element_type=jnp.fl...  52.4 us
    psum x4, blocking collectives, on_device(): length = lax.psum(jnp.sum(updated * updated), 'sec')  49.6 us
    convert_element_type x4, other arithmetic, on_device(): lowered = vector.astype(jnp.bfloat16)  34.2 us
  transfers between devices with their start and end apart: 11, of which 5 were waited for; matrix products, arithmetic and copies ran while one was open for 11% of the time, Pallas kernels for 0%

commit v1 on v0

v1 whole, which is shorter than its diff:
```python
import functools
import jax
import jax.numpy as jnp
from jax import lax
from jax.experimental import pallas as pl
from jax.experimental.pallas import tpu as pltpu
from jax.sharding import PartitionSpec as P

ITERS = 4
STATES = 4


def from_behind(shard, axis, by):
    count = lax.axis_size(axis)
    pairs = [(i, i + by) for i in range(count) if 0 <= i + by < count]
    return lax.ppermute(shard, axis, pairs)


def couple_and_mix(part_ref, coupling_ref, operator_ref, out_ref):
    coupling = coupling_ref[0]
    operator = operator_ref[0]
    for at in range(part_ref.shape[0]):
        u = lax.dot_general(
            part_ref[at], coupling, (((1,), (1,)), ((), ())), preferred_element_type=jnp.float32
        ).astype(jnp.bfloat16)
        out_ref[0, at] = jnp.dot(operator, u, preferred_element_type=jnp.float32).astype(
            jnp.bfloat16
        )


def own_block(lowered, couplings, operators):
    bond_size, pair_count, row_count = lowered.shape
    flops = 2 * bond_size * pair_count * row_count * (row_count + pair_count)
    return pl.pallas_call(
        couple_and_mix,
        out_shape=jax.ShapeDtypeStruct((3,) + lowered.shape, jnp.bfloat16),
        grid=(bond_size // STATES,),
        in_specs=[
            pl.BlockSpec((STATES, pair_count, row_count), lambda i: (i, 0, 0)),
            pl.BlockSpec((1, row_count, row_count), lambda i: (1, 0, 0)),
            pl.BlockSpec((1, pair_count, pair_count), lambda i: (1, 0, 0)),
        ],
        out_specs=pl.BlockSpec((1, STATES, pair_count, row_count), lambda i: (1, i, 0, 0)),
        compiler_params=pltpu.CompilerParams(vmem_limit_bytes=32 * 2**20),
        cost_estimate=pl.CostEstimate(
            flops=flops, bytes_accessed=4 * lowered.size, transcendentals=0
        ),
    )(lowered, couplings, operators)


def side_kernel(half, relay, detour_ref, *refs):
    parts, (coupling_ref, operator_ref, _, out_ref) = refs[:-4], refs[-4:]
    side, step = pl.program_id(0), pl.program_id(1)
    other = detour_ref[side] == 1
    run = lambda ref: couple_and_mix(ref, coupling_ref, operator_ref, out_ref)
    straight = jnp.logical_not(other)
    pl.when(jnp.logical_and(straight, side == 0))(lambda: run(parts[0]))
    pl.when(jnp.logical_and(straight, side == 1))(lambda: run(parts[1]))
    if relay:
        pl.when(jnp.logical_and(other, step < half))(lambda: run(parts[2]))
        pl.when(jnp.logical_and(other, step >= half))(lambda: run(parts[3]))


def side_blocks(detour, parts, couplings, operators, mixed):
    bond_size, pair_count, row_count = mixed.shape[1:]
    steps = bond_size // STATES
    half = steps // 2
    relay = len(parts) == 4
    block = (STATES, pair_count, row_count)

    def low(k, i, detour_ref):
        return (jnp.where((k == 0) & (detour_ref[0] == 0), i, steps - 1), 0, 0)

    def high(k, i, detour_ref):
        return (jnp.where((k == 1) & (detour_ref[1] == 0), i, 0), 0, 0)

    def first(k, i, detour_ref):
        return (jnp.where(detour_ref[k] == 1, jnp.minimum(i, half - 1), 0), 0, 0)

    def second(k, i, detour_ref):
        return (jnp.where(detour_ref[k] == 1, jnp.maximum(i - half, 0), 0), 0, 0)

    maps = [low, high, first, second][: len(parts)]
    flops = 4 * bond_size * pair_count * row_count * (row_count + pair_count)
    return pl.pallas_call(
        functools.partial(side_kernel, half, relay),
        out_shape=jax.ShapeDtypeStruct(mixed.shape, mixed.dtype),
        grid_spec=pltpu.PrefetchScalarGridSpec(
            num_scalar_prefetch=1,
            grid=(2, steps),
            in_specs=[pl.BlockSpec(block, at) for at in maps]
            + [
                pl.BlockSpec((1, row_count, row_count), lambda k, i, d: (2 * k, 0, 0)),
                pl.BlockSpec((1, pair_count, pair_count), lambda k, i, d: (2 * k, 0, 0)),
                pl.BlockSpec(memory_space=pl.ANY),
            ],
            out_specs=pl.BlockSpec((1,) + block, lambda k, i, d: (2 * k, i, 0, 0)),
        ),
        input_output_aliases={len(parts) + 3: 0},
        compiler_params=pltpu.CompilerParams(vmem_limit_bytes=32 * 2**20),
        cost_estimate=pl.CostEstimate(
            flops=flops, bytes_accessed=8 * bond_size * pair_count * row_count, transcendentals=0
        ),
    )(detour, *parts, couplings, operators, mixed)


def exchange(lowered, place):
    count = lax.axis_size("sec")
    forward = [(i, i + 1) for i in range(count - 1)]
    if count != 8:
        low = lax.ppermute(lowered, "sec", forward)
        high = lax.ppermute(lowered, "sec", [(b, a) for a, b in forward])
        return [low, high], jnp.zeros((2,), jnp.int32)
    half = lowered.shape[0] // 2
    leg = lax.ppermute(lowered[:half], "sec", [(3, 7), (4, 0)])
    straight = lax.ppermute(lowered[half:], "sec", [(3, 4), (4, 3)])
    forward.remove((3, 4))
    low = lax.ppermute(lowered, "sec", forward)
    high = lax.ppermute(lowered, "sec", [(b, a) for a, b in forward])
    round_by = lax.ppermute(leg, "sec", [(7, 4), (0, 3)])
    detour = jnp.stack([place == 4, place == 3]).astype(jnp.int32)
    return [low, high, round_by, straight], detour


def advance(tensors, operators, environ):
    highest = lax.Precision.HIGHEST
    first = jnp.einsum("cpx,kxy->kcpy", tensors, environ, precision=highest)
    second = jnp.einsum("kcpy,kpz->kczy", first, operators, precision=highest)
    return jnp.einsum("kczy,bzy->kcb", second, tensors, precision=highest)


def on_device(psi_start, left_blocks, site_ops, site_tensors, env_ops, boundary, precond):
    tensors_here = site_tensors[0]
    operators_here = env_ops[0]
    position_sect = lax.axis_index("sect")
    place = lax.axis_index("sec")
    final_sect = lax.axis_size("sect") - 1
    current = advance(tensors_here, operators_here, boundary)
    for step in range(lax.axis_size("sect") - 1):
        received = from_behind(current, "sect", -1)
        current = jnp.where(
            position_sect == final_sect, current, advance(tensors_here, operators_here, received)
        )
    kept = jnp.transpose(psi_start[0], (1, 2, 0))
    inverse = 1.0 / jnp.transpose(precond[0], (1, 2, 0))
    environ = current.astype(jnp.bfloat16)
    operators = site_ops[0]
    couplings = left_blocks[0, :, 0]
    cell_count = kept.size * lax.axis_size("sec")
    ritz_value = jnp.float32(0.0)
    scale = jnp.float32(1.0)
    lowered = kept.astype(jnp.bfloat16)
    for iteration in range(ITERS):
        parts, detour = exchange(lowered, place)
        mixed = own_block(lowered, couplings, operators)
        mixed = side_blocks(detour, parts, couplings, operators, mixed)
        image = jnp.einsum("kcb,kbtr->ctr", environ, mixed, preferred_element_type=jnp.float32)
        small = image * (1.0 / 64.0)
        intersection, norm_sq, size = lax.psum(
            (jnp.sum(kept * image), jnp.sum(kept * kept), jnp.sum(small * small)), "sec"
        )
        if iteration:
            scale = scale * lax.rsqrt(scale * scale * (norm_sq / cell_count) + 1e-06)
        ritz_value = intersection / norm_sq
        factor = lax.rsqrt((norm_sq + size) / cell_count)
        kept = (kept - (image - ritz_value * kept) * inverse) * factor
        lowered = kept.astype(jnp.bfloat16)
        scale = scale / factor
    norm_sq = lax.psum(jnp.sum(kept * kept), "sec")
    scale = scale * lax.rsqrt(scale * scale * (norm_sq / cell_count) + 1e-06)
    vector = jnp.transpose(kept * scale, (2, 0, 1))
    return (vector[None], jnp.reshape(ritz_value, (1,)))


def solution(mesh):
    placed = (
        P("sect", "sec", None, None),
        P("sect", None, None, "sec", None),
        P("sect", None, None, None),
        P("sect", "sec", None, None),
        P("sect", None, None, None),
        P(None, "sec", None),
        P("sect", "sec", None, None),
    )
    return jax.shard_map(
        on_device,
        mesh=mesh,
        in_specs=placed,
        out_specs=(P("sect", "sec", None, None), P("sect")),
        check_vma=False,
    )
```

time: 1050 us -> 907 us (0.86)
  blocking collectives: 549 us -> 66.8 us
  waiting for transfers between devices: 11.4 us -> 303 us
  matrix products: 251 us -> 105 us
  Pallas kernels: 0 us -> 136 us
  local copies, waits for them, and re-layouts: 13.8 us -> 47.5 us
  starting transfers between devices: 25.5 us -> 56.5 us
    psum x8 -> x5, blocking collectives: 549 us -> 66.8 us  [the longest x4 53.7 us: on_device(): lax.psum((jnp.sum(kept * image), jnp.sum(kept * kept), jnp.sum(small * sm...]
    ppermute x8 -> x20, waiting for transfers between devices: 1.2 us -> 294 us  [the longest x4 172 us: exchange(): round_by = lax.ppermute(leg, 'sec', [(7, 4), (0, 3)])]
    dot_general x20 -> x4, matrix products: 207 us -> 60.8 us  [on_device(): jnp.einsum('kcb,kbtr->ctr', environ, mixed, preferred_element_type=jnp.fl...]
    pallas_call x0 -> x8, Pallas kernels: none -> 136 us  [the longest x4 91.3 us: side_blocks(): pl.pallas_call(functools.partial(side_kernel, half, relay), out_shape=jax...]
    reduce_sum x8 -> x5, other arithmetic: 132 us -> 67.2 us  [the longest x4 52.3 us: on_device(): jnp.sum(kept * image)]
    convert_element_type x4 -> x5, other arithmetic: 34.2 us -> 64.8 us  [the longest x4 64.7 us: on_device(): lowered = kept.astype(jnp.bfloat16)]
    ppermute x8 -> x20, starting transfers between devices: 21.2 us -> 51.4 us  [the longest x4 21.6 us: exchange(): low = lax.ppermute(lowered, 'sec', forward)]
    broadcast_in_dim x1, other arithmetic: 10.6 us -> 36.9 us  [on_device(): return (vector[None], jnp.reshape(ritz_value, (1,)))]
  transfers between devices with their start and end apart: 11 -> 23, of which waited for: 5 -> 9; matrix products, arithmetic and copies ran while one was open for 11% -> 6% of each run, Pallas kernels for 0% -> 5%
where the time goes in v1:
time: 907 us; the launch traced here: 899 us
  waiting for transfers between devices  303 us (33%)
  other arithmetic  169 us (19%)
  Pallas kernels  136 us (15%)
  matrix products  105 us (12%)
  blocking collectives  66.8 us (7%)
  starting transfers between devices  56.5 us (6%)
  local copies, waits for them, and re-layouts  47.5 us (5%)
  between operations  15.4 us (2%)
    ppermute x4, waiting for transfers between devices, exchange(): round_by = lax.ppermute(leg, 'sec', [(7, 4), (0, 3)])  172 us
    ppermute x4, waiting for transfers between devices, exchange(): leg = lax.ppermute(lowered[:half], 'sec', [(3, 7), (4, 0)])  121 us
    pallas_call x4, Pallas kernels, side_blocks(): pl.pallas_call(functools.partial(side_kernel, half, relay), out_shape=jax...  91.3 us
    convert_element_type x4, other arithmetic, on_device(): lowered = kept.astype(jnp.bfloat16)  64.7 us
    dot_general x4, matrix products, on_device(): jnp.einsum('kcb,kbtr->ctr', environ, mixed, preferred_element_type=jnp.fl...  60.8 us
    psum x4, blocking collectives, on_device(): lax.psum((jnp.sum(kept * image), jnp.sum(kept * kept), jnp.sum(small * sm...  53.7 us
    reduce_sum x4, other arithmetic, on_device(): jnp.sum(kept * image)  52.3 us
    pallas_call x4, Pallas kernels, own_block(): pl.pallas_call(couple_and_mix, out_shape=jax.ShapeDtypeStruct((3,) + lowe...  44.6 us
  transfers between devices with their start and end apart: 23, of which 9 were waited for; matrix products, arithmetic and copies ran while one was open for 6% of the time, Pallas kernels for 5%

profile of v1, /device:TPU:0, one launch (start us, length us, event | category | flops | bytes accessed | tf_op | source)
XLA Modules:
  0.0 898.7 jit_solution(10689690390441134312)
XLA Ops:
  0.7 8.2 bitcast_convert_fusion.part_ref
  8.9 6.1 fusion.96
  17.7 6.8 collective-permute-start.3
  24.5 2.3 collective-permute-start.7
  26.8 2.7 fusion.73
  31.3 24.9 %collective-permute-done.5 = bf16[16,400,256]{2,1,0:T(8,128)(2,1)} collective-permute-done((bf16[16,400,256]{2,1,0:T(8,128)(2,1)}, bf16[16,400,256]{2,1,0:T(8,128)(2,1)}, u32[]{:S(2)}, u32[]{:S(2)}) %collective-permute-start.5) | collective-permute-done | bytes 3276832 | tf_op jit(solution)/shard_map/ppermute | solution.py:115
  56.3 3.8 collective-permute-start.6
  60.1 7.2 fusion.52
  71.4 4.4 collective-permute-done
  75.8 2.7 fusion.70
  80.4 7.2 fusion.50
  91.8 12.2 %shard_map.86.refs_6_ = bf16[3,32,400,256]{3,2,1,0:T(8,128)(2,1)} custom-call(bf16[32,400,256]{2,1,0:T(8,128)(2,1)} %bitcast_convert_fusion.part_ref, bf16[3,256,256]{2,1,0:T(8,128)(2,1)S(1)} %bitcast.233, bf16[3,400,400]{2,1,0:T(8,128)(2,1)S(1)} %bitcast.225), custom_call_target="tpu_custom_call" | custom-call | flops 4299161600 | bytes 13107200 | tf_op jit(solution)/shard_map/pallas_call | solution.py:34
  104.0 2.7 fusion.67
  108.5 7.2 fusion.48
  120.3 4.7 collective-permute-done.2
  124.9 2.7 fusion.64
  129.5 8.0 fusion.46
  140.1 24.3 %shard_map.87 = bf16[3,32,400,256]{3,2,1,0:T(8,128)(2,1)} custom-call(s32[2]{0:T(128)S(1)} %add_convert_fusion.detour_ref, bf16[32,400,256]{2,1,0:T(8,128)(2,1)} %collective-permute-done.3.refs_0_, bf16[32,400,256]{2,1,0:T(8,128)(2,1)} %collective-permute-done.4.refs_1_, ...), custom_call_target="tpu_custom_call", output_to_operand_aliasing={{}: (7, {})} | custom-call | flops 8598323200 | bytes 26214400 | tf_op jit(solution)/shard_map/pallas_call | solution.py:85
  164.4 15.3 %multiply_reduce_fusion.9 = (f32[]{:T(128)}, f32[32,400,256]{2,0,1:T(8,128)}) fusion(bf16[3,32,32,1]{2,1,0,3:T(8,128)(2,1)S(1)} %fusion.58, bf16[3,32,400,256]{3,2,1,0:T(8,128)(2,1)} %shard_map.87), kind=kOutput, calls=%fused_computation.57 | convolution fusion | flops 638976000 | bytes 32774148 | tf_op jit(solution)/shard_map/kcb,kbtr->ctr/dot_general | solution.py:157
  179.6 16.3 %fusion.31 = (f32[]{:T(128)}, f32[]{:T(128)}) fusion(f32[1,256,32,400]{1,3,2,0:T(8,128)} %param.7, f32[32,400,256]{2,0,1:T(8,128)} %get-tuple-element.37), kind=kLoop, calls=%fused_computation.43 | loop fusion | flops 13107198 | bytes 26214408 | tf_op jit(solution)/shard_map/reduce_sum | solution.py:160
  195.9 12.9 %all-reduce.3 = (f32[]{:T(128)}, f32[]{:T(128)}, f32[]{:T(128)}) all-reduce(f32[]{:T(128)} %get-tuple-element.9, f32[]{:T(128)} %get-tuple-element.36, f32[]{:T(128)} %get-tuple-element.8), channel_id=1, replica_groups=mesh['sect'=4,'sec'=8] {'sec'}, use_global_device_ids=true, to_apply=%region_3.4 | all-reduce | flops 3 | bytes 24 | tf_op jit(solution)/shard_map/psum | solution.py:159
  211.6 18.3 %fusion.91 = (bf16[32,400,256]{2,1,0:T(8,128)(2,1)S(1)}, f32[32,400,256]{2,1,0:T(8,128)}) fusion(f32[]{:T(128)S(6)} %rsqrt.24, f32[1,256,32,400]{1,3,2,0:T(8,128)} %param.13, f32[]{:T(128)S(6)} %div.62, f32[32,400,256]{2,0,1:T(8,128)} %get-tuple-element.37, f32[1,256,32,400]{1,3,2,0:T(8,128)} %param.7), kind=kLoop, calls=%fused_computation.111 | loop fusion | flops 22937600 | bytes 58982408 | tf_op jit(solution)/shard_map/convert_element_type | solution.py:167
  229.8 2.1 fusion.95
  234.5 3.8 collective-permute-start.8
  239.2 33.6 %collective-permute-done.10 = bf16[16,400,256]{2,1,0:T(8,128)(2,1)} collective-permute-done((bf16[16,400,256]{2,1,0:T(8,128)(2,1)}, bf16[16,400,256]{2,1,0:T(8,128)(2,1)}, u32[]{:S(2)}, u32[]{:S(2)}) %collective-permute-start.10) | collective-permute-done | bytes 3276832 | tf_op jit(solution)/shard_map/ppermute | solution.py:115
  272.8 3.0 collective-permute-start.11
  275.8 9.9 %shard_map.88.refs_6_ = bf16[3,32,400,256]{3,2,1,0:T(8,128)(2,1)} custom-call(bf16[32,400,256]{2,1,0:T(8,128)(2,1)S(1)} %get-tuple-element.26.part_ref, bf16[3,256,256]{2,1,0:T(8,128)(2,1)S(1)} %bitcast.235, bf16[3,400,400]{2,1,0:T(8,128)(2,1)S(1)} %bitcast.227), custom_call_target="tpu_custom_call" | custom-call | flops 4299161600 | bytes 13107200 | tf_op jit(solution)/shard_map/pallas_call | solution.py:34
  287.4 58.1 %collective-permute-done.11.refs_2_ = bf16[16,400,256]{2,1,0:T(8,128)(2,1)} collective-permute-done((bf16[16,400,256]{2,1,0:T(8,128)(2,1)}, bf16[16,400,256]{2,1,0:T(8,128)(2,1)}, u32[]{:S(2)}, u32[]{:S(2)}) %collective-permute-start.11) | collective-permute-done | bytes 3276832 | tf_op jit(solution)/shard_map/ppermute | solution.py:120
  345.5 2.7 copy-done.4
  348.2 2.9 copy-done.5
  351.0 1.9 copy-done.9
  353.0 21.4 %shard_map.89 = bf16[3,32,400,256]{3,2,1,0:T(8,128)(2,1)} custom-call(s32[2]{0:T(128)S(1)} %add_convert_fusion.detour_ref, bf16[32,400,256]{2,1,0:T(8,128)(2,1)S(1)} %copy-done.5, bf16[32,400,256]{2,1,0:T(8,128)(2,1)S(1)} %collective-permute-done.9.refs_1_, bf16[16,400,256]{2,1,0:T(8,128)(2,1)} %collective-permute-done.11.refs_2_, ...), custom_call_target="tpu_custom_call", output_to_operand_aliasing={{}: (7, {})} | custom-call | flops 8598323200 | bytes 26214400 | tf_op jit(solution)/shard_map/pallas_call | solution.py:85
  374.4 15.3 %multiply_reduce_fusion.6 = (f32[]{:T(128)}, f32[32,400,256]{2,0,1:T(8,128)}) fusion(bf16[3,32,32,1]{2,1,0,3:T(8,128)(2,1)S(1)} %fusion.58, bf16[3,32,400,256]{3,2,1,0:T(8,128)(2,1)} %shard_map.89), kind=kOutput, calls=%fused_computation.54 | convolution fusion | flops 638976000 | bytes 32774148 | tf_op jit(solution)/shard_map/kcb,kbtr->ctr/dot_general | solution.py:157
  389.7 12.0 %multiply_reduce_fusion.8 = (f32[]{:T(128)}, f32[]{:T(128)}) fusion(f32[32,400,256]{2,1,0:T(8,128)} %get-tuple-element.27, f32[32,400,256]{2,0,1:T(8,128)} %get-tuple-element.39), kind=kLoop, calls=%fused_computation.56 | loop fusion | flops 13107198 | bytes 26214408 | tf_op jit(solution)/shard_map/reduce_sum | solution.py:160
  401.7 13.6 %all-reduce.2 = (f32[]{:T(128)}, f32[]{:T(128)}, f32[]{:T(128)}) all-reduce(f32[]{:T(128)} %get-tuple-element.7, f32[]{:T(128)} %get-tuple-element.38, f32[]{:T(128)} %get-tuple-element.6), channel_id=1, replica_groups=mesh['sect'=4,'sec'=8] {'sec'}, use_global_device_ids=true, to_apply=%region_9.10 | all-reduce | flops 3 | bytes 24 | tf_op jit(solution)/shard_map/psum | solution.py:159
  417.8 18.2 %fusion.89 = (bf16[32,400,256]{2,1,0:T(8,128)(2,1)S(1)}, f32[32,400,256]{2,1,0:T(8,128)}) fusion(f32[]{:T(128)S(6)} %rsqrt.25, f32[32,400,256]{2,1,0:T(8,128)} %get-tuple-element.27, f32[1,256,32,400]{1,3,2,0:T(8,128)} %param.13, f32[]{:T(128)S(6)} %div.68, f32[32,400,256]{2,0,1:T(8,128)} %get-tuple-element.39), kind=kLoop, calls=%fused_computation.110 | loop fusion | flops 22937600 | bytes 58982408 | tf_op jit(solution)/shard_map/convert_element_type | solution.py:167
  436.0 2.1 fusion.94
  440.7 4.4 collective-permute-start.13
  446.0 33.2 %collective-permute-done.15 = bf16[16,400,256]{2,1,0:T(8,128)(2,1)} collective-permute-done((bf16[16,400,256]{2,1,0:T(8,128)(2,1)}, bf16[16,400,256]{2,1,0:T(8,128)(2,1)}, u32[]{:S(2)}, u32[]{:S(2)}) %collective-permute-start.15) | collective-permute-done | bytes 3276832 | tf_op jit(solution)/shard_map/ppermute | solution.py:115
  479.2 3.0 collective-permute-start.16
  482.2 9.9 %shard_map.90.refs_6_ = bf16[3,32,400,256]{3,2,1,0:T(8,128)(2,1)} custom-call(bf16[32,400,256]{2,1,0:T(8,128)(2,1)S(1)} %get-tuple-element.24.part_ref, bf16[3,256,256]{2,1,0:T(8,128)(2,1)S(1)} %bitcast.237, bf16[3,400,400]{2,1,0:T(8,128)(2,1)S(1)} %bitcast.229), custom_call_target="tpu_custom_call" | custom-call | flops 4299161600 | bytes 13107200 | tf_op jit(solution)/shard_map/pallas_call | solution.py:34
  493.9 58.3 %collective-permute-done.16.refs_2_ = bf16[16,400,256]{2,1,0:T(8,128)(2,1)} collective-permute-done((bf16[16,400,256]{2,1,0:T(8,128)(2,1)}, bf16[16,400,256]{2,1,0:T(8,128)(2,1)}, u32[]{:S(2)}, u32[]{:S(2)}) %collective-permute-start.16) | collective-permute-done | bytes 3276832 | tf_op jit(solution)/shard_map/ppermute | solution.py:120
  552.2 2.7 copy-done.6
  554.9 2.9 copy-done.7
  557.7 1.9 copy-done.11
  559.7 21.4 %shard_map.91 = bf16[3,32,400,256]{3,2,1,0:T(8,128)(2,1)} custom-call(s32[2]{0:T(128)S(1)} %add_convert_fusion.detour_ref, bf16[32,400,256]{2,1,0:T(8,128)(2,1)S(1)} %copy-done.7, bf16[32,400,256]{2,1,0:T(8,128)(2,1)S(1)} %collective-permute-done.14.refs_1_, bf16[16,400,256]{2,1,0:T(8,128)(2,1)} %collective-permute-done.16.refs_2_, ...), custom_call_target="tpu_custom_call", output_to_operand_aliasing={{}: (7, {})} | custom-call | flops 8598323200 | bytes 26214400 | tf_op jit(solution)/shard_map/pallas_call | solution.py:85
  581.1 15.1 %multiply_reduce_fusion.3 = (f32[]{:T(128)}, f32[32,400,256]{2,0,1:T(8,128)}) fusion(bf16[3,32,32,1]{2,1,0,3:T(8,128)(2,1)S(1)} %fusion.58, bf16[3,32,400,256]{3,2,1,0:T(8,128)(2,1)} %shard_map.91), kind=kOutput, calls=%fused_computation.51 | convolution fusion | flops 638976000 | bytes 32774148 | tf_op jit(solution)/shard_map/kcb,kbtr->ctr/dot_general | solution.py:157
  596.3 12.0 %multiply_reduce_fusion.5 = (f32[]{:T(128)}, f32[]{:T(128)}) fusion(f32[32,400,256]{2,1,0:T(8,128)} %get-tuple-element.25, f32[32,400,256]{2,0,1:T(8,128)} %get-tuple-element.41), kind=kLoop, calls=%fused_computation.53 | loop fusion | flops 13107198 | bytes 26214408 | tf_op jit(solution)/shard_map/reduce_sum | solution.py:160
  608.2 13.2 %all-reduce.1 = (f32[]{:T(128)}, f32[]{:T(128)}, f32[]{:T(128)}) all-reduce(f32[]{:T(128)} %get-tuple-element.5, f32[]{:T(128)} %get-tuple-element.40, f32[]{:T(128)} %get-tuple-element.4), channel_id=1, replica_groups=mesh['sect'=4,'sec'=8] {'sec'}, use_global_device_ids=true, to_apply=%region_15.16 | all-reduce | flops 3 | bytes 24 | tf_op jit(solution)/shard_map/psum | solution.py:159
  624.0 20.0 %fusion.87 = (bf16[32,400,256]{2,1,0:T(8,128)(2,1)}, f32[32,400,256]{2,1,0:T(8,128)}) fusion(f32[]{:T(128)S(6)} %rsqrt.26, f32[32,400,256]{2,1,0:T(8,128)} %get-tuple-element.25, f32[1,256,32,400]{1,3,2,0:T(8,128)} %param.13, f32[]{:T(128)S(6)} %div.70, f32[32,400,256]{2,0,1:T(8,128)} %get-tuple-element.41), kind=kLoop, calls=%fused_computation.109 | loop fusion | flops 22937600 | bytes 58982408 | tf_op jit(solution)/shard_map/convert_element_type | solution.py:167
  644.0 5.1 fusion.93
  651.7 6.6 collective-permute-start.18
  658.3 2.3 collective-permute-start.22
  660.6 29.7 %collective-permute-done.20 = bf16[16,400,256]{2,1,0:T(8,128)(2,1)} collective-permute-done((bf16[16,400,256]{2,1,0:T(8,128)(2,1)S(1)}, bf16[16,400,256]{2,1,0:T(8,128)(2,1)}, u32[]{:S(2)}, u32[]{:S(2)}) %collective-permute-start.20) | collective-permute-done | bytes 3276832 | tf_op jit(solution)/shard_map/ppermute | solution.py:115
  690.4 3.1 collective-permute-start.21
  694.9 12.6 %shard_map.92.refs_6_ = bf16[3,32,400,256]{3,2,1,0:T(8,128)(2,1)} custom-call(bf16[32,400,256]{2,1,0:T(8,128)(2,1)} %get-tuple-element.22.part_ref, bf16[3,256,256]{2,1,0:T(8,128)(2,1)S(1)} %bitcast.239, bf16[3,400,400]{2,1,0:T(8,128)(2,1)S(1)} %bitcast.231), custom_call_target="tpu_custom_call" | custom-call | flops 4299161600 | bytes 13107200 | tf_op jit(solution)/shard_map/pallas_call | solution.py:34
  707.5 55.8 %collective-permute-done.21.refs_2_ = bf16[16,400,256]{2,1,0:T(8,128)(2,1)} collective-permute-done((bf16[16,400,256]{2,1,0:T(8,128)(2,1)}, bf16[16,400,256]{2,1,0:T(8,128)(2,1)}, u32[]{:S(2)}, u32[]{:S(2)}) %collective-permute-start.21) | collective-permute-done | bytes 3276832 | tf_op jit(solution)/shard_map/ppermute | solution.py:120
  763.3 24.1 %shard_map.93 = bf16[3,32,400,256]{3,2,1,0:T(8,128)(2,1)} custom-call(s32[2]{0:T(128)S(1)} %add_convert_fusion.detour_ref, bf16[32,400,256]{2,1,0:T(8,128)(2,1)} %collective-permute-done.18.refs_0_, bf16[32,400,256]{2,1,0:T(8,128)(2,1)} %collective-permute-done.19.refs_1_, ...), custom_call_target="tpu_custom_call", output_to_operand_aliasing={{}: (7, {})} | custom-call | flops 8598323200 | bytes 26214400 | tf_op jit(solution)/shard_map/pallas_call | solution.py:85
  787.5 15.1 %multiply_reduce_fusion = (f32[]{:T(128)}, f32[32,400,256]{2,0,1:T(8,128)}) fusion(bf16[3,32,32,1]{2,1,0,3:T(8,128)(2,1)S(1)} %fusion.58, bf16[3,32,400,256]{3,2,1,0:T(8,128)(2,1)} %shard_map.93), kind=kOutput, calls=%fused_computation.48 | convolution fusion | flops 638976000 | bytes 32774148 | tf_op jit(solution)/shard_map/kcb,kbtr->ctr/dot_general | solution.py:157
  802.6 12.1 %multiply_reduce_fusion.2 = (f32[]{:T(128)}, f32[]{:T(128)}) fusion(f32[32,400,256]{2,1,0:T(8,128)} %get-tuple-element.23, f32[32,400,256]{2,0,1:T(8,128)} %get-tuple-element.43), kind=kLoop, calls=%fused_computation.50 | loop fusion | flops 13107198 | bytes 26214408 | tf_op jit(solution)/shard_map/reduce_sum | solution.py:160
  814.7 13.9 %all-reduce = (f32[]{:T(128)}, f32[]{:T(128)}, f32[]{:T(128)}) all-reduce(f32[]{:T(128)} %get-tuple-element.3, f32[]{:T(128)} %get-tuple-element.42, f32[]{:T(128)} %get-tuple-element.2), channel_id=1, replica_groups=mesh['sect'=4,'sec'=8] {'sec'}, use_global_device_ids=true, to_apply=%region_21.22 | all-reduce | flops 3 | bytes 24 | tf_op jit(solution)/shard_map/psum | solution.py:159
  831.8 14.9 %fusion.25 = f32[]{:T(128)} fusion(f32[32,400,256]{2,1,0:T(8,128)} %get-tuple-element.23, f32[32,400,256]{2,0,1:T(8,128)} %get-tuple-element.43, f32[]{:T(128)S(6)} %rsqrt.27, f32[]{:T(128)} %div.72, f32[1,256,32,400]{1,3,2,0:T(8,128)} %param.13), kind=kLoop, calls=%fused_computation.31 | loop fusion | flops 26214400 | bytes 39321612 | tf_op jit(solution)/shard_map/reduce_sum | solution.py:169
  846.6 13.1 %psum.103 = f32[]{:T(128)} all-reduce(f32[]{:T(128)} %fusion.25), channel_id=1, replica_groups=mesh['sect'=4,'sec'=8] {'sec'}, use_global_device_ids=true, to_apply=%region_25.26 | all-reduce | flops 1 | bytes 8 | tf_op jit(solution)/shard_map/psum | solution.py:169
  860.4 36.9 %fusion.12 = f32[1,256,32,400]{1,3,2,0:T(8,128)} fusion(f32[1,256,32,400]{1,3,2,0:T(8,128)} %param.7, f32[32,400,256]{2,0,1:T(8,128)} %get-tuple-element.43, f32[32,400,256]{2,0,1:T(8,128)} %get-tuple-element.41, f32[32,400,256]{2,0,1:T(8,128)} %get-tuple-element.39, f32[32,400,256]{2,0,1:T(8,128)} %get-tuple-element.37, f32[]{:T(128)S(6)} %mul.274, ...), kind=kLoop, calls=%fused_computation.13 | loop fusion | flops 72089600 | bytes 91750432 | tf_op jit(solution)/shard_map/broadcast_in_dim | solution.py:172
  (68 shorter events, 38.3 us)
Async XLA Ops:
  0.6 26.2 %copy-start = (f32[1,32,20,32]{3,1,2,0:T(8,128)S(1)}, f32[1,32,20,32]{3,1,2,0:T(8,128)}, u32[]{:S(2)}) copy-start(f32[1,32,20,32]{3,1,2,0:T(8,128)} %param.10) | copy-start | bytes 245764
  0.6 26.1 %copy-start.16 = (f32[3,32,32]{2,1,0:T(8,128)S(1)}, f32[3,32,32]{2,1,0:T(8,128)}, u32[]{:S(2)}) copy-start(f32[3,32,32]{2,1,0:T(8,128)} %param.12) | copy-start | bytes 36868
  8.9 51.2 %copy-start.12 = (f32[1,3,20,20]{3,0,2,1:T(1,128)S(1)}, f32[1,3,20,20]{3,0,2,1:T(1,128)}, u32[]{:S(2)}) copy-start(f32[1,3,20,20]{3,0,2,1:T(1,128)} %param.11) | copy-start | bytes 14404
  14.9 76.8 %copy-start.2 = (bf16[1,3,400,400]{3,2,1,0:T(8,128)(2,1)S(1)}, bf16[1,3,400,400]{3,2,1,0:T(8,128)(2,1)}, u32[]{:S(2)}) copy-start(bf16[1,3,400,400]{3,2,1,0:T(8,128)(2,1)} %param.9) | copy-start | bytes 2880004
  14.9 76.8 %copy-start.3 = (bf16[1,3,1,256,256]{4,3,2,1,0:T(8,128)(2,1)S(1)}, bf16[1,3,1,256,256]{4,3,2,1,0:T(8,128)(2,1)}, u32[]{:S(2)}) copy-start(bf16[1,3,1,256,256]{4,3,2,1,0:T(8,128)(2,1)} %param.8) | copy-start | bytes 1179652
  14.9 41.3 %collective-permute-start.5 = (bf16[16,400,256]{2,1,0:T(8,128)(2,1)}, bf16[16,400,256]{2,1,0:T(8,128)(2,1)}, u32[]{:S(2)}, u32[]{:S(2)}) collective-permute-start(bf16[16,400,256]{2,1,0:T(8,128)(2,1)} %get-tuple-element.35), channel_id=1, source_target_pairs={{3,7},{4,0},{11,15},{12,8},{19,23},{20,16},{27,31},{28,24}} | collective-permute-start | bytes 9830408 | tf_op jit(solution)/shard_map/ppermute | solution.py:115
  16.4 123.7 %collective-permute-start.4 = (bf16[32,400,256]{2,1,0:T(8,128)(2,1)}, bf16[32,400,256]{2,1,0:T(8,128)(2,1)}, u32[]{:S(2)}, u32[]{:S(2)}) collective-permute-start(bf16[32,400,256]{2,1,0:T(8,128)(2,1)} %bitcast_convert_fusion.part_ref), channel_id=1, source_target_pairs={{1,0},{2,1},{3,2},{5,4},{6,5},{7,6},{9,8},{10,9},{11,10},{13,12},{... | collective-permute-start | bytes 19660808 | tf_op jit(solution)/shard_map/ppermute | solution.py:119
  17.7 122.4 %collective-permute-start.3 = (bf16[32,400,256]{2,1,0:T(8,128)(2,1)}, bf16[32,400,256]{2,1,0:T(8,128)(2,1)}, u32[]{:S(2)}, u32[]{:S(2)}) collective-permute-start(bf16[32,400,256]{2,1,0:T(8,128)(2,1)} %bitcast_convert_fusion.part_ref), channel_id=1, source_target_pairs={{0,1},{1,2},{2,3},{4,5},{5,6},{6,7},{8,9},{9,10},{10,11},{12,13},{... | collective-permute-start | bytes 19660808 | tf_op jit(solution)/shard_map/ppermute | solution.py:118
  24.5 115.5 %collective-permute-start.7 = (bf16[16,400,256]{2,1,0:T(8,128)(2,1)}, bf16[16,400,256]{2,1,0:T(8,128)(2,1)}, u32[]{:S(2)}, u32[]{:S(2)}) collective-permute-start(bf16[16,400,256]{2,1,0:T(8,128)(2,1)} %get-tuple-element.34), channel_id=1, source_target_pairs={{3,4},{4,3},{11,12},{12,11},{19,20},{20,19},{27,28},{28,27}} | collective-permute-start | bytes 9830408 | tf_op jit(solution)/shard_map/ppermute | solution.py:116
  56.3 83.8 %collective-permute-start.6 = (bf16[16,400,256]{2,1,0:T(8,128)(2,1)}, bf16[16,400,256]{2,1,0:T(8,128)(2,1)}, u32[]{:S(2)}, u32[]{:S(2)}) collective-permute-start(bf16[16,400,256]{2,1,0:T(8,128)(2,1)} %collective-permute-done.5), channel_id=1, source_target_pairs={{7,4},{0,3},{15,12},{8,11},{23,20},{16,19},{31,28},{24,27}} | collective-permute-start | bytes 9830408 | tf_op jit(solution)/shard_map/ppermute | solution.py:120
  69.8 6.0 copy-start.15
  69.8 6.0 collective-permute-start
  90.1 13.9 %copy-start.13 = (f32[3,32,32]{2,1,0:T(8,128)}, f32[3,32,32]{2,1,0:T(8,128)S(1)}, u32[]{:S(2)}) copy-start(f32[3,32,32]{2,1,0:T(8,128)S(1)} %fusion.54) | copy-start | bytes 36868
  90.1 13.9 %collective-permute-start.1 = (f32[3,32,32]{2,1,0:T(8,128)S(1)}, f32[3,32,32]{2,1,0:T(8,128)S(1)}, u32[]{:S(2)}, u32[]{:S(2)}) collective-permute-start(f32[3,32,32]{2,1,0:T(8,128)S(1)} %fusion.54), channel_id=1, source_target_pairs={{8,0},{16,8},{24,16},{9,1},{17,9},{25,17},{10,2},{18,10},{26,18},{... | collective-permute-start | bytes 36872 | tf_op jit(solution)/shard_map/ppermute | solution.py:16
  118.3 6.6 copy-start.14
  118.3 6.6 collective-permute-start.2
  231.9 40.9 %collective-permute-start.10 = (bf16[16,400,256]{2,1,0:T(8,128)(2,1)}, bf16[16,400,256]{2,1,0:T(8,128)(2,1)}, u32[]{:S(2)}, u32[]{:S(2)}) collective-permute-start(bf16[16,400,256]{2,1,0:T(8,128)(2,1)} %get-tuple-element.33), channel_id=1, source_target_pairs={{3,7},{4,0},{11,15},{12,8},{19,23},{20,16},{27,31},{28,24}} | collective-permute-start | bytes 9830408 | tf_op jit(solution)/shard_map/ppermute | solution.py:115
  233.2 112.2 %collective-permute-start.9 = (bf16[32,400,256]{2,1,0:T(8,128)(2,1)S(1)}, bf16[32,400,256]{2,1,0:T(8,128)(2,1)S(1)}, u32[]{:S(2)}, u32[]{:S(2)}) collective-permute-start(bf16[32,400,256]{2,1,0:T(8,128)(2,1)S(1)} %get-tuple-element.26.part_ref), channel_id=1, source_target_pairs={{1,0},{2,1},{3,2},{5,4},{6,5},{7,6},{9,8},{10,9},{11,10},{13,12},{... | collective-permute-start | bytes 19660808 | tf_op jit(solution)/shard_map/ppermute | solution.py:119
  234.5 110.9 %collective-permute-start.8 = (bf16[32,400,256]{2,1,0:T(8,128)(2,1)S(1)}, bf16[32,400,256]{2,1,0:T(8,128)(2,1)S(1)}, u32[]{:S(2)}, u32[]{:S(2)}) collective-permute-start(bf16[32,400,256]{2,1,0:T(8,128)(2,1)S(1)} %get-tuple-element.26.part_ref), channel_id=1, source_target_pairs={{0,1},{1,2},{2,3},{4,5},{5,6},{6,7},{8,9},{9,10},{10,11},{12,13},{... | collective-permute-start | bytes 19660808 | tf_op jit(solution)/shard_map/ppermute | solution.py:118
  238.3 47.4 %collective-permute-start.12 = (bf16[16,400,256]{2,1,0:T(8,128)(2,1)S(1)}, bf16[16,400,256]{2,1,0:T(8,128)(2,1)S(1)}, u32[]{:S(2)}, u32[]{:S(2)}) collective-permute-start(bf16[16,400,256]{2,1,0:T(8,128)(2,1)S(1)} %get-tuple-element.32), channel_id=1, source_target_pairs={{3,4},{4,3},{11,12},{12,11},{19,20},{20,19},{27,28},{28,27}} | collective-permute-start | bytes 9830408 | tf_op jit(solution)/shard_map/ppermute | solution.py:116
  272.8 72.6 %collective-permute-start.11 = (bf16[16,400,256]{2,1,0:T(8,128)(2,1)}, bf16[16,400,256]{2,1,0:T(8,128)(2,1)}, u32[]{:S(2)}, u32[]{:S(2)}) collective-permute-start(bf16[16,400,256]{2,1,0:T(8,128)(2,1)} %collective-permute-done.10), channel_id=1, source_target_pairs={{7,4},{0,3},{15,12},{8,11},{23,20},{16,19},{31,28},{24,27}} | collective-permute-start | bytes 9830408 | tf_op jit(solution)/shard_map/ppermute | solution.py:120
  285.7 1.7 copy-start.8
  345.5 2.7 copy-start.4
  348.2 2.9 copy-start.5
  351.0 1.9 copy-start.9
  438.1 41.1 %collective-permute-start.15 = (bf16[16,400,256]{2,1,0:T(8,128)(2,1)}, bf16[16,400,256]{2,1,0:T(8,128)(2,1)}, u32[]{:S(2)}, u32[]{:S(2)}) collective-permute-start(bf16[16,400,256]{2,1,0:T(8,128)(2,1)} %get-tuple-element.31), channel_id=1, source_target_pairs={{3,7},{4,0},{11,15},{12,8},{19,23},{20,16},{27,31},{28,24}} | collective-permute-start | bytes 9830408 | tf_op jit(solution)/shard_map/ppermute | solution.py:115
  439.4 112.7 %collective-permute-start.14 = (bf16[32,400,256]{2,1,0:T(8,128)(2,1)S(1)}, bf16[32,400,256]{2,1,0:T(8,128)(2,1)S(1)}, u32[]{:S(2)}, u32[]{:S(2)}) collective-permute-start(bf16[32,400,256]{2,1,0:T(8,128)(2,1)S(1)} %get-tuple-element.24.part_ref), channel_id=1, source_target_pairs={{1,0},{2,1},{3,2},{5,4},{6,5},{7,6},{9,8},{10,9},{11,10},{13,12},{... | collective-permute-start | bytes 19660808 | tf_op jit(solution)/shard_map/ppermute | solution.py:119
  440.7 111.4 %collective-permute-start.13 = (bf16[32,400,256]{2,1,0:T(8,128)(2,1)S(1)}, bf16[32,400,256]{2,1,0:T(8,128)(2,1)S(1)}, u32[]{:S(2)}, u32[]{:S(2)}) collective-permute-start(bf16[32,400,256]{2,1,0:T(8,128)(2,1)S(1)} %get-tuple-element.24.part_ref), channel_id=1, source_target_pairs={{0,1},{1,2},{2,3},{4,5},{5,6},{6,7},{8,9},{9,10},{10,11},{12,13},{... | collective-permute-start | bytes 19660808 | tf_op jit(solution)/shard_map/ppermute | solution.py:118
  445.1 47.0 %collective-permute-start.17 = (bf16[16,400,256]{2,1,0:T(8,128)(2,1)S(1)}, bf16[16,400,256]{2,1,0:T(8,128)(2,1)S(1)}, u32[]{:S(2)}, u32[]{:S(2)}) collective-permute-start(bf16[16,400,256]{2,1,0:T(8,128)(2,1)S(1)} %get-tuple-element.30), channel_id=1, source_target_pairs={{3,4},{4,3},{11,12},{12,11},{19,20},{20,19},{27,28},{28,27}} | collective-permute-start | bytes 9830408 | tf_op jit(solution)/shard_map/ppermute | solution.py:116
  479.2 72.9 %collective-permute-start.16 = (bf16[16,400,256]{2,1,0:T(8,128)(2,1)}, bf16[16,400,256]{2,1,0:T(8,128)(2,1)}, u32[]{:S(2)}, u32[]{:S(2)}) collective-permute-start(bf16[16,400,256]{2,1,0:T(8,128)(2,1)} %collective-permute-done.15), channel_id=1, source_target_pairs={{7,4},{0,3},{15,12},{8,11},{23,20},{16,19},{31,28},{24,27}} | collective-permute-start | bytes 9830408 | tf_op jit(solution)/shard_map/ppermute | solution.py:120
  492.1 1.7 copy-start.10
  552.2 2.7 copy-start.6
  554.9 2.9 copy-start.7
  557.7 1.9 copy-start.11
  649.1 41.3 %collective-permute-start.20 = (bf16[16,400,256]{2,1,0:T(8,128)(2,1)S(1)}, bf16[16,400,256]{2,1,0:T(8,128)(2,1)}, u32[]{:S(2)}, u32[]{:S(2)}) collective-permute-start(bf16[16,400,256]{2,1,0:T(8,128)(2,1)S(1)} %get-tuple-element.29), channel_id=1, source_target_pairs={{3,7},{4,0},{11,15},{12,8},{19,23},{20,16},{27,31},{28,24}} | collective-permute-start | bytes 9830408 | tf_op jit(solution)/shard_map/ppermute | solution.py:115
  650.4 113.0 %collective-permute-start.19 = (bf16[32,400,256]{2,1,0:T(8,128)(2,1)}, bf16[32,400,256]{2,1,0:T(8,128)(2,1)}, u32[]{:S(2)}, u32[]{:S(2)}) collective-permute-start(bf16[32,400,256]{2,1,0:T(8,128)(2,1)} %get-tuple-element.22.part_ref), channel_id=1, source_target_pairs={{1,0},{2,1},{3,2},{5,4},{6,5},{7,6},{9,8},{10,9},{11,10},{13,12},{... | collective-permute-start | bytes 19660808 | tf_op jit(solution)/shard_map/ppermute | solution.py:119
  651.7 111.7 %collective-permute-start.18 = (bf16[32,400,256]{2,1,0:T(8,128)(2,1)}, bf16[32,400,256]{2,1,0:T(8,128)(2,1)}, u32[]{:S(2)}, u32[]{:S(2)}) collective-permute-start(bf16[32,400,256]{2,1,0:T(8,128)(2,1)} %get-tuple-element.22.part_ref), channel_id=1, source_target_pairs={{0,1},{1,2},{2,3},{4,5},{5,6},{6,7},{8,9},{9,10},{10,11},{12,13},{... | collective-permute-start | bytes 19660808 | tf_op jit(solution)/shard_map/ppermute | solution.py:118
  658.3 49.2 %collective-permute-start.22 = (bf16[16,400,256]{2,1,0:T(8,128)(2,1)}, bf16[16,400,256]{2,1,0:T(8,128)(2,1)}, u32[]{:S(2)}, u32[]{:S(2)}) collective-permute-start(bf16[16,400,256]{2,1,0:T(8,128)(2,1)} %get-tuple-element.28), channel_id=1, source_target_pairs={{3,4},{4,3},{11,12},{12,11},{19,20},{20,19},{27,28},{28,27}} | collective-permute-start | bytes 9830408 | tf_op jit(solution)/shard_map/ppermute | solution.py:116
  690.4 73.0 %collective-permute-start.21 = (bf16[16,400,256]{2,1,0:T(8,128)(2,1)}, bf16[16,400,256]{2,1,0:T(8,128)(2,1)}, u32[]{:S(2)}, u32[]{:S(2)}) collective-permute-start(bf16[16,400,256]{2,1,0:T(8,128)(2,1)} %collective-permute-done.20), channel_id=1, source_target_pairs={{7,4},{0,3},{15,12},{8,11},{23,20},{16,19},{31,28},{24,27}} | collective-permute-start | bytes 9830408 | tf_op jit(solution)/shard_map/ppermute | solution.py:120
  860.4 37.0 %copy-start.1 = (f32[1,32,20,32]{3,1,2,0:T(8,128)S(1)}, f32[1,32,20,32]{3,1,2,0:T(8,128)}, u32[]{:S(2)}) copy-start(f32[1,32,20,32]{3,1,2,0:T(8,128)} %param.10) | copy-start | bytes 245764

commit v2 on v1

--- a/solution.py
+++ b/solution.py
@@ -166,7 +166,8 @@
         kept = (kept - (image - ritz_value * kept) * inverse) * factor
         lowered = kept.astype(jnp.bfloat16)
         scale = scale / factor
-    norm_sq = lax.psum(jnp.sum(kept * kept), "sec")
+    kept, local_sq = lax.optimization_barrier((kept, jnp.sum(kept * kept)))
+    norm_sq = lax.psum(local_sq, "sec")
     scale = scale * lax.rsqrt(scale * scale * (norm_sq / cell_count) + 1e-06)
     vector = jnp.transpose(kept * scale, (2, 0, 1))
     return (vector[None], jnp.reshape(ritz_value, (1,)))

time: 907 us -> 886 us (0.977)
  other arithmetic: 169 us -> 147 us
    broadcast_in_dim x1, other arithmetic: 36.9 us -> 10.6 us  [on_device(): return (vector[None], jnp.reshape(ritz_value, (1,)))]
  transfers between devices with their start and end apart: 23 -> 23, of which waited for: 9 -> 9; matrix products, arithmetic and copies ran while one was open for 6% -> 7% of each run, Pallas kernels for 5% -> 5%
where the time goes in v2:
time: 886 us; the launch traced here: 878 us
  waiting for transfers between devices  303 us (34%)
  other arithmetic  147 us (17%)
  Pallas kernels  136 us (15%)
  matrix products  105 us (12%)
  blocking collectives  66.9 us (8%)
  starting transfers between devices  56.1 us (6%)
  local copies, waits for them, and re-layouts  47.7 us (5%)
  between operations  16.6 us (2%)
    ppermute x4, waiting for transfers between devices, exchange(): round_by = lax.ppermute(leg, 'sec', [(7, 4), (0, 3)])  172 us
    ppermute x4, waiting for transfers between devices, exchange(): leg = lax.ppermute(lowered[:half], 'sec', [(3, 7), (4, 0)])  121 us
    pallas_call x4, Pallas kernels, side_blocks(): pl.pallas_call(functools.partial(side_kernel, half, relay), out_shape=jax...  91.3 us
    convert_element_type x4, other arithmetic, on_device(): lowered = kept.astype(jnp.bfloat16)  64.7 us
    dot_general x4, matrix products, on_device(): jnp.einsum('kcb,kbtr->ctr', environ, mixed, preferred_element_type=jnp.fl...  60.8 us
    psum x4, blocking collectives, on_device(): lax.psum((jnp.sum(kept * image), jnp.sum(kept * kept), jnp.sum(small * sm...  53.8 us
    reduce_sum x4, other arithmetic, on_device(): jnp.sum(kept * image)  52.2 us
    pallas_call x4, Pallas kernels, own_block(): pl.pallas_call(couple_and_mix, out_shape=jax.ShapeDtypeStruct((3,) + lowe...  44.4 us
  transfers between devices with their start and end apart: 23, of which 9 were waited for; matrix products, arithmetic and copies ran while one was open for 7% of the time, Pallas kernels for 5%

profile of v2, /device:TPU:0, one launch (start us, length us, event | category | flops | bytes accessed | tf_op | source)
XLA Modules:
  0.0 877.5 jit_solution(9883429220269479295)
XLA Ops:
  0.7 8.2 bitcast_convert_fusion.part_ref
  8.9 6.1 fusion.82
  17.6 6.8 collective-permute-start.3
  24.5 2.3 collective-permute-start.7
  26.8 2.7 fusion.58
  31.4 24.9 %collective-permute-done.5 = bf16[16,400,256]{2,1,0:T(8,128)(2,1)} collective-permute-done((bf16[16,400,256]{2,1,0:T(8,128)(2,1)}, bf16[16,400,256]{2,1,0:T(8,128)(2,1)}, u32[]{:S(2)}, u32[]{:S(2)}) %collective-permute-start.5) | collective-permute-done | bytes 3276832 | tf_op jit(solution)/shard_map/ppermute | solution.py:115
  56.3 3.8 collective-permute-start.6
  60.1 7.2 fusion.37
  71.3 4.5 collective-permute-done
  75.8 2.7 fusion.55
  80.3 7.2 fusion.35
  91.7 12.2 %shard_map.86.refs_6_ = bf16[3,32,400,256]{3,2,1,0:T(8,128)(2,1)} custom-call(bf16[32,400,256]{2,1,0:T(8,128)(2,1)} %bitcast_convert_fusion.part_ref, bf16[3,256,256]{2,1,0:T(8,128)(2,1)S(1)} %bitcast.174, bf16[3,400,400]{2,1,0:T(8,128)(2,1)S(1)} %bitcast.166), custom_call_target="tpu_custom_call" | custom-call | flops 4299161600 | bytes 13107200 | tf_op jit(solution)/shard_map/pallas_call | solution.py:34
  103.9 2.7 fusion.52
  108.5 7.2 fusion.33
  120.1 4.8 collective-permute-done.2
  124.9 2.7 fusion.49
  129.4 8.0 fusion.31
  140.0 24.3 %shard_map.87 = bf16[3,32,400,256]{3,2,1,0:T(8,128)(2,1)} custom-call(s32[2]{0:T(128)S(1)} %add_convert_fusion.detour_ref, bf16[32,400,256]{2,1,0:T(8,128)(2,1)} %collective-permute-done.3.refs_0_, bf16[32,400,256]{2,1,0:T(8,128)(2,1)} %collective-permute-done.4.refs_1_, ...), custom_call_target="tpu_custom_call", output_to_operand_aliasing={{}: (7, {})} | custom-call | flops 8598323200 | bytes 26214400 | tf_op jit(solution)/shard_map/pallas_call | solution.py:85
  164.3 15.2 %multiply_reduce_fusion.10 = (f32[]{:T(128)}, f32[32,400,256]{2,0,1:T(8,128)}) fusion(bf16[3,32,32,1]{2,1,0,3:T(8,128)(2,1)S(1)} %fusion.43, bf16[3,32,400,256]{3,2,1,0:T(8,128)(2,1)} %shard_map.87), kind=kOutput, calls=%fused_computation.38 | convolution fusion | flops 638976000 | bytes 32774148 | tf_op jit(solution)/shard_map/kcb,kbtr->ctr/dot_general | solution.py:157
  179.5 16.4 %fusion.16 = (f32[]{:T(128)}, f32[]{:T(128)}) fusion(f32[1,256,32,400]{1,3,2,0:T(8,128)} %param.7, f32[32,400,256]{2,0,1:T(8,128)} %get-tuple-element.43), kind=kLoop, calls=%fused_computation.24 | loop fusion | flops 13107198 | bytes 26214408 | tf_op jit(solution)/shard_map/reduce_sum | solution.py:160
  195.9 12.9 %all-reduce.3 = (f32[]{:T(128)}, f32[]{:T(128)}, f32[]{:T(128)}) all-reduce(f32[]{:T(128)} %get-tuple-element.13, f32[]{:T(128)} %get-tuple-element.42, f32[]{:T(128)} %get-tuple-element.12), channel_id=1, replica_groups=mesh['sect'=4,'sec'=8] {'sec'}, use_global_device_ids=true, to_apply=%region_3.4 | all-reduce | flops 3 | bytes 24 | tf_op jit(solution)/shard_map/psum | solution.py:159
  211.5 18.2 %fusion.77 = (bf16[32,400,256]{2,1,0:T(8,128)(2,1)S(1)}, f32[32,400,256]{2,1,0:T(8,128)}) fusion(f32[]{:T(128)S(6)} %rsqrt.24, f32[1,256,32,400]{1,3,2,0:T(8,128)} %param.13, f32[]{:T(128)S(6)} %div.60, f32[32,400,256]{2,0,1:T(8,128)} %get-tuple-element.43, f32[1,256,32,400]{1,3,2,0:T(8,128)} %param.7), kind=kLoop, calls=%fused_computation.92 | loop fusion | flops 22937600 | bytes 58982408 | tf_op jit(solution)/shard_map/convert_element_type | solution.py:167
  229.7 2.1 fusion.81
  234.4 3.8 collective-permute-start.8
  239.1 33.6 %collective-permute-done.10 = bf16[16,400,256]{2,1,0:T(8,128)(2,1)} collective-permute-done((bf16[16,400,256]{2,1,0:T(8,128)(2,1)}, bf16[16,400,256]{2,1,0:T(8,128)(2,1)}, u32[]{:S(2)}, u32[]{:S(2)}) %collective-permute-start.10) | collective-permute-done | bytes 3276832 | tf_op jit(solution)/shard_map/ppermute | solution.py:115
  272.7 2.9 collective-permute-start.11
  275.7 9.9 %shard_map.88.refs_6_ = bf16[3,32,400,256]{3,2,1,0:T(8,128)(2,1)} custom-call(bf16[32,400,256]{2,1,0:T(8,128)(2,1)S(1)} %get-tuple-element.32.part_ref, bf16[3,256,256]{2,1,0:T(8,128)(2,1)S(1)} %bitcast.176, bf16[3,400,400]{2,1,0:T(8,128)(2,1)S(1)} %bitcast.168), custom_call_target="tpu_custom_call" | custom-call | flops 4299161600 | bytes 13107200 | tf_op jit(solution)/shard_map/pallas_call | solution.py:34
  287.3 58.1 %collective-permute-done.11.refs_2_ = bf16[16,400,256]{2,1,0:T(8,128)(2,1)} collective-permute-done((bf16[16,400,256]{2,1,0:T(8,128)(2,1)}, bf16[16,400,256]{2,1,0:T(8,128)(2,1)}, u32[]{:S(2)}, u32[]{:S(2)}) %collective-permute-start.11) | collective-permute-done | bytes 3276832 | tf_op jit(solution)/shard_map/ppermute | solution.py:120
  345.4 2.8 copy-done.4
  348.2 2.9 copy-done.5
  351.0 1.9 copy-done.9
  353.0 21.4 %shard_map.89 = bf16[3,32,400,256]{3,2,1,0:T(8,128)(2,1)} custom-call(s32[2]{0:T(128)S(1)} %add_convert_fusion.detour_ref, bf16[32,400,256]{2,1,0:T(8,128)(2,1)S(1)} %copy-done.5, bf16[32,400,256]{2,1,0:T(8,128)(2,1)S(1)} %collective-permute-done.9.refs_1_, bf16[16,400,256]{2,1,0:T(8,128)(2,1)} %collective-permute-done.11.refs_2_, ...), custom_call_target="tpu_custom_call", output_to_operand_aliasing={{}: (7, {})} | custom-call | flops 8598323200 | bytes 26214400 | tf_op jit(solution)/shard_map/pallas_call | solution.py:85
  374.4 15.2 %multiply_reduce_fusion.7 = (f32[]{:T(128)}, f32[32,400,256]{2,0,1:T(8,128)}) fusion(bf16[3,32,32,1]{2,1,0,3:T(8,128)(2,1)S(1)} %fusion.43, bf16[3,32,400,256]{3,2,1,0:T(8,128)(2,1)} %shard_map.89), kind=kOutput, calls=%fused_computation.35 | convolution fusion | flops 638976000 | bytes 32774148 | tf_op jit(solution)/shard_map/kcb,kbtr->ctr/dot_general | solution.py:157
  389.6 12.0 %multiply_reduce_fusion.9 = (f32[]{:T(128)}, f32[]{:T(128)}) fusion(f32[32,400,256]{2,1,0:T(8,128)} %get-tuple-element.33, f32[32,400,256]{2,0,1:T(8,128)} %get-tuple-element.45), kind=kLoop, calls=%fused_computation.37 | loop fusion | flops 13107198 | bytes 26214408 | tf_op jit(solution)/shard_map/reduce_sum | solution.py:160
  401.6 13.7 %all-reduce.2 = (f32[]{:T(128)}, f32[]{:T(128)}, f32[]{:T(128)}) all-reduce(f32[]{:T(128)} %get-tuple-element.11, f32[]{:T(128)} %get-tuple-element.44, f32[]{:T(128)} %get-tuple-element.10), channel_id=1, replica_groups=mesh['sect'=4,'sec'=8] {'sec'}, use_global_device_ids=true, to_apply=%region_9.10 | all-reduce | flops 3 | bytes 24 | tf_op jit(solution)/shard_map/psum | solution.py:159
  418.0 18.2 %fusion.75 = (bf16[32,400,256]{2,1,0:T(8,128)(2,1)S(1)}, f32[32,400,256]{2,1,0:T(8,128)}) fusion(f32[]{:T(128)S(6)} %rsqrt.25, f32[32,400,256]{2,1,0:T(8,128)} %get-tuple-element.33, f32[1,256,32,400]{1,3,2,0:T(8,128)} %param.13, f32[]{:T(128)S(6)} %div.66, f32[32,400,256]{2,0,1:T(8,128)} %get-tuple-element.45), kind=kLoop, calls=%fused_computation.91 | loop fusion | flops 22937600 | bytes 58982408 | tf_op jit(solution)/shard_map/convert_element_type | solution.py:167
  436.3 2.1 fusion.80
  441.0 4.4 collective-permute-start.13
  446.3 33.2 %collective-permute-done.15 = bf16[16,400,256]{2,1,0:T(8,128)(2,1)} collective-permute-done((bf16[16,400,256]{2,1,0:T(8,128)(2,1)}, bf16[16,400,256]{2,1,0:T(8,128)(2,1)}, u32[]{:S(2)}, u32[]{:S(2)}) %collective-permute-start.15) | collective-permute-done | bytes 3276832 | tf_op jit(solution)/shard_map/ppermute | solution.py:115
  479.5 3.0 collective-permute-start.16
  482.5 9.9 %shard_map.90.refs_6_ = bf16[3,32,400,256]{3,2,1,0:T(8,128)(2,1)} custom-call(bf16[32,400,256]{2,1,0:T(8,128)(2,1)S(1)} %get-tuple-element.30.part_ref, bf16[3,256,256]{2,1,0:T(8,128)(2,1)S(1)} %bitcast.178, bf16[3,400,400]{2,1,0:T(8,128)(2,1)S(1)} %bitcast.170), custom_call_target="tpu_custom_call" | custom-call | flops 4299161600 | bytes 13107200 | tf_op jit(solution)/shard_map/pallas_call | solution.py:34
  494.1 58.3 %collective-permute-done.16.refs_2_ = bf16[16,400,256]{2,1,0:T(8,128)(2,1)} collective-permute-done((bf16[16,400,256]{2,1,0:T(8,128)(2,1)}, bf16[16,400,256]{2,1,0:T(8,128)(2,1)}, u32[]{:S(2)}, u32[]{:S(2)}) %collective-permute-start.16) | collective-permute-done | bytes 3276832 | tf_op jit(solution)/shard_map/ppermute | solution.py:120
  552.4 2.8 copy-done.6
  555.2 2.9 copy-done.7
  558.1 1.9 copy-done.11
  560.0 21.4 %shard_map.91 = bf16[3,32,400,256]{3,2,1,0:T(8,128)(2,1)} custom-call(s32[2]{0:T(128)S(1)} %add_convert_fusion.detour_ref, bf16[32,400,256]{2,1,0:T(8,128)(2,1)S(1)} %copy-done.7, bf16[32,400,256]{2,1,0:T(8,128)(2,1)S(1)} %collective-permute-done.14.refs_1_, bf16[16,400,256]{2,1,0:T(8,128)(2,1)} %collective-permute-done.16.refs_2_, ...), custom_call_target="tpu_custom_call", output_to_operand_aliasing={{}: (7, {})} | custom-call | flops 8598323200 | bytes 26214400 | tf_op jit(solution)/shard_map/pallas_call | solution.py:85
  581.4 15.2 %multiply_reduce_fusion.4 = (f32[]{:T(128)}, f32[32,400,256]{2,0,1:T(8,128)}) fusion(bf16[3,32,32,1]{2,1,0,3:T(8,128)(2,1)S(1)} %fusion.43, bf16[3,32,400,256]{3,2,1,0:T(8,128)(2,1)} %shard_map.91), kind=kOutput, calls=%fused_computation.32 | convolution fusion | flops 638976000 | bytes 32774148 | tf_op jit(solution)/shard_map/kcb,kbtr->ctr/dot_general | solution.py:157
  596.6 11.9 %multiply_reduce_fusion.6 = (f32[]{:T(128)}, f32[]{:T(128)}) fusion(f32[32,400,256]{2,1,0:T(8,128)} %get-tuple-element.31, f32[32,400,256]{2,0,1:T(8,128)} %get-tuple-element.47), kind=kLoop, calls=%fused_computation.34 | loop fusion | flops 13107198 | bytes 26214408 | tf_op jit(solution)/shard_map/reduce_sum | solution.py:160
  608.6 13.3 %all-reduce.1 = (f32[]{:T(128)}, f32[]{:T(128)}, f32[]{:T(128)}) all-reduce(f32[]{:T(128)} %get-tuple-element.9, f32[]{:T(128)} %get-tuple-element.46, f32[]{:T(128)} %get-tuple-element.8), channel_id=1, replica_groups=mesh['sect'=4,'sec'=8] {'sec'}, use_global_device_ids=true, to_apply=%region_15.16 | all-reduce | flops 3 | bytes 24 | tf_op jit(solution)/shard_map/psum | solution.py:159
  624.6 20.0 %fusion.73 = (bf16[32,400,256]{2,1,0:T(8,128)(2,1)}, f32[32,400,256]{2,1,0:T(8,128)}) fusion(f32[]{:T(128)S(6)} %rsqrt.26, f32[32,400,256]{2,1,0:T(8,128)} %get-tuple-element.31, f32[1,256,32,400]{1,3,2,0:T(8,128)} %param.13, f32[]{:T(128)S(6)} %div.68, f32[32,400,256]{2,0,1:T(8,128)} %get-tuple-element.47), kind=kLoop, calls=%fused_computation.90 | loop fusion | flops 22937600 | bytes 58982408 | tf_op jit(solution)/shard_map/convert_element_type | solution.py:167
  644.6 5.1 fusion.79
  652.2 6.6 collective-permute-start.18
  658.8 2.4 collective-permute-start.22
  661.2 29.7 %collective-permute-done.20 = bf16[16,400,256]{2,1,0:T(8,128)(2,1)} collective-permute-done((bf16[16,400,256]{2,1,0:T(8,128)(2,1)S(1)}, bf16[16,400,256]{2,1,0:T(8,128)(2,1)}, u32[]{:S(2)}, u32[]{:S(2)}) %collective-permute-start.20) | collective-permute-done | bytes 3276832 | tf_op jit(solution)/shard_map/ppermute | solution.py:115
  690.9 3.0 collective-permute-start.21
  695.5 12.4 %shard_map.92.refs_6_ = bf16[3,32,400,256]{3,2,1,0:T(8,128)(2,1)} custom-call(bf16[32,400,256]{2,1,0:T(8,128)(2,1)} %get-tuple-element.28.part_ref, bf16[3,256,256]{2,1,0:T(8,128)(2,1)S(1)} %bitcast.180, bf16[3,400,400]{2,1,0:T(8,128)(2,1)S(1)} %bitcast.172), custom_call_target="tpu_custom_call" | custom-call | flops 4299161600 | bytes 13107200 | tf_op jit(solution)/shard_map/pallas_call | solution.py:34
  707.9 55.9 %collective-permute-done.21.refs_2_ = bf16[16,400,256]{2,1,0:T(8,128)(2,1)} collective-permute-done((bf16[16,400,256]{2,1,0:T(8,128)(2,1)}, bf16[16,400,256]{2,1,0:T(8,128)(2,1)}, u32[]{:S(2)}, u32[]{:S(2)}) %collective-permute-start.21) | collective-permute-done | bytes 3276832 | tf_op jit(solution)/shard_map/ppermute | solution.py:120
  763.8 24.1 %shard_map.93 = bf16[3,32,400,256]{3,2,1,0:T(8,128)(2,1)} custom-call(s32[2]{0:T(128)S(1)} %add_convert_fusion.detour_ref, bf16[32,400,256]{2,1,0:T(8,128)(2,1)} %collective-permute-done.18.refs_0_, bf16[32,400,256]{2,1,0:T(8,128)(2,1)} %collective-permute-done.19.refs_1_, ...), custom_call_target="tpu_custom_call", output_to_operand_aliasing={{}: (7, {})} | custom-call | flops 8598323200 | bytes 26214400 | tf_op jit(solution)/shard_map/pallas_call | solution.py:85
  788.0 15.2 %multiply_reduce_fusion.1 = (f32[]{:T(128)}, f32[32,400,256]{2,0,1:T(8,128)}) fusion(bf16[3,32,32,1]{2,1,0,3:T(8,128)(2,1)S(1)} %fusion.43, bf16[3,32,400,256]{3,2,1,0:T(8,128)(2,1)} %shard_map.93), kind=kOutput, calls=%fused_computation.29 | convolution fusion | flops 638976000 | bytes 32774148 | tf_op jit(solution)/shard_map/kcb,kbtr->ctr/dot_general | solution.py:157
  803.1 12.0 %multiply_reduce_fusion.3 = (f32[]{:T(128)}, f32[]{:T(128)}) fusion(f32[32,400,256]{2,1,0:T(8,128)} %get-tuple-element.29, f32[32,400,256]{2,0,1:T(8,128)} %get-tuple-element.49), kind=kLoop, calls=%fused_computation.31 | loop fusion | flops 13107198 | bytes 26214408 | tf_op jit(solution)/shard_map/reduce_sum | solution.py:160
  815.1 14.0 %all-reduce = (f32[]{:T(128)}, f32[]{:T(128)}, f32[]{:T(128)}) all-reduce(f32[]{:T(128)} %get-tuple-element.7, f32[]{:T(128)} %get-tuple-element.48, f32[]{:T(128)} %get-tuple-element.6), channel_id=1, replica_groups=mesh['sect'=4,'sec'=8] {'sec'}, use_global_device_ids=true, to_apply=%region_21.22 | all-reduce | flops 3 | bytes 24 | tf_op jit(solution)/shard_map/psum | solution.py:159
  832.6 19.0 %multiply_reduce_fusion = (f32[]{:T(128)}, f32[32,400,256]{2,1,0:T(8,128)}) fusion(f32[]{:T(128)S(6)} %rsqrt.27, f32[32,400,256]{2,1,0:T(8,128)} %get-tuple-element.29, f32[1,256,32,400]{1,3,2,0:T(8,128)} %param.13, f32[]{:T(128)} %div.70, f32[32,400,256]{2,0,1:T(8,128)} %get-tuple-element.49), kind=kLoop, calls=%fused_computation.28 | loop fusion | flops 26214400 | bytes 52428812 | tf_op jit(solution)/shard_map/reduce_sum | solution.py:169
  851.5 13.1 %psum.103 = f32[]{:T(128)} all-reduce(f32[]{:T(128)} %get-tuple-element.5), channel_id=1, replica_groups=mesh['sect'=4,'sec'=8] {'sec'}, use_global_device_ids=true, to_apply=%region_25.26 | all-reduce | flops 1 | bytes 8 | tf_op jit(solution)/shard_map/psum | solution.py:170
  865.3 10.6 %multiply_bitcast_fusion = f32[1,256,32,400]{1,3,2,0:T(8,128)} fusion(f32[32,400,256]{2,1,0:T(8,128)} %get-tuple-element.4, f32[]{:T(128)S(6)} %mul.201), kind=kLoop, calls=%fused_computation.27 | loop fusion | flops 3276800 | bytes 26214404 | tf_op jit(solution)/shard_map/broadcast_in_dim | solution.py:173
  (68 shorter events, 38.0 us)
Async XLA Ops:
  0.6 26.2 %copy-start = (f32[1,32,20,32]{3,1,2,0:T(8,128)S(1)}, f32[1,32,20,32]{3,1,2,0:T(8,128)}, u32[]{:S(2)}) copy-start(f32[1,32,20,32]{3,1,2,0:T(8,128)} %param.10) | copy-start | bytes 245764
  0.6 26.1 %copy-start.16 = (f32[3,32,32]{2,1,0:T(8,128)S(1)}, f32[3,32,32]{2,1,0:T(8,128)}, u32[]{:S(2)}) copy-start(f32[3,32,32]{2,1,0:T(8,128)} %param.12) | copy-start | bytes 36868
  8.9 51.2 %copy-start.12 = (f32[1,3,20,20]{3,0,2,1:T(1,128)S(1)}, f32[1,3,20,20]{3,0,2,1:T(1,128)}, u32[]{:S(2)}) copy-start(f32[1,3,20,20]{3,0,2,1:T(1,128)} %param.11) | copy-start | bytes 14404
  14.9 76.8 %copy-start.2 = (bf16[1,3,400,400]{3,2,1,0:T(8,128)(2,1)S(1)}, bf16[1,3,400,400]{3,2,1,0:T(8,128)(2,1)}, u32[]{:S(2)}) copy-start(bf16[1,3,400,400]{3,2,1,0:T(8,128)(2,1)} %param.9) | copy-start | bytes 2880004
  14.9 76.8 %copy-start.3 = (bf16[1,3,1,256,256]{4,3,2,1,0:T(8,128)(2,1)S(1)}, bf16[1,3,1,256,256]{4,3,2,1,0:T(8,128)(2,1)}, u32[]{:S(2)}) copy-start(bf16[1,3,1,256,256]{4,3,2,1,0:T(8,128)(2,1)} %param.8) | copy-start | bytes 1179652
  14.9 41.3 %collective-permute-start.5 = (bf16[16,400,256]{2,1,0:T(8,128)(2,1)}, bf16[16,400,256]{2,1,0:T(8,128)(2,1)}, u32[]{:S(2)}, u32[]{:S(2)}) collective-permute-start(bf16[16,400,256]{2,1,0:T(8,128)(2,1)} %get-tuple-element.41), channel_id=1, source_target_pairs={{3,7},{4,0},{11,15},{12,8},{19,23},{20,16},{27,31},{28,24}} | collective-permute-start | bytes 9830408 | tf_op jit(solution)/shard_map/ppermute | solution.py:115
  16.3 123.6 %collective-permute-start.4 = (bf16[32,400,256]{2,1,0:T(8,128)(2,1)}, bf16[32,400,256]{2,1,0:T(8,128)(2,1)}, u32[]{:S(2)}, u32[]{:S(2)}) collective-permute-start(bf16[32,400,256]{2,1,0:T(8,128)(2,1)} %bitcast_convert_fusion.part_ref), channel_id=1, source_target_pairs={{1,0},{2,1},{3,2},{5,4},{6,5},{7,6},{9,8},{10,9},{11,10},{13,12},{... | collective-permute-start | bytes 19660808 | tf_op jit(solution)/shard_map/ppermute | solution.py:119
  17.6 122.3 %collective-permute-start.3 = (bf16[32,400,256]{2,1,0:T(8,128)(2,1)}, bf16[32,400,256]{2,1,0:T(8,128)(2,1)}, u32[]{:S(2)}, u32[]{:S(2)}) collective-permute-start(bf16[32,400,256]{2,1,0:T(8,128)(2,1)} %bitcast_convert_fusion.part_ref), channel_id=1, source_target_pairs={{0,1},{1,2},{2,3},{4,5},{5,6},{6,7},{8,9},{9,10},{10,11},{12,13},{... | collective-permute-start | bytes 19660808 | tf_op jit(solution)/shard_map/ppermute | solution.py:118
  24.5 115.5 %collective-permute-start.7 = (bf16[16,400,256]{2,1,0:T(8,128)(2,1)}, bf16[16,400,256]{2,1,0:T(8,128)(2,1)}, u32[]{:S(2)}, u32[]{:S(2)}) collective-permute-start(bf16[16,400,256]{2,1,0:T(8,128)(2,1)} %get-tuple-element.40), channel_id=1, source_target_pairs={{3,4},{4,3},{11,12},{12,11},{19,20},{20,19},{27,28},{28,27}} | collective-permute-start | bytes 9830408 | tf_op jit(solution)/shard_map/ppermute | solution.py:116
  56.3 83.7 %collective-permute-start.6 = (bf16[16,400,256]{2,1,0:T(8,128)(2,1)}, bf16[16,400,256]{2,1,0:T(8,128)(2,1)}, u32[]{:S(2)}, u32[]{:S(2)}) collective-permute-start(bf16[16,400,256]{2,1,0:T(8,128)(2,1)} %collective-permute-done.5), channel_id=1, source_target_pairs={{7,4},{0,3},{15,12},{8,11},{23,20},{16,19},{31,28},{24,27}} | collective-permute-start | bytes 9830408 | tf_op jit(solution)/shard_map/ppermute | solution.py:120
  69.8 6.0 copy-start.15
  69.8 6.0 collective-permute-start
  90.1 13.8 %copy-start.13 = (f32[3,32,32]{2,1,0:T(8,128)}, f32[3,32,32]{2,1,0:T(8,128)S(1)}, u32[]{:S(2)}) copy-start(f32[3,32,32]{2,1,0:T(8,128)S(1)} %fusion.39) | copy-start | bytes 36868
  90.1 13.8 %collective-permute-start.1 = (f32[3,32,32]{2,1,0:T(8,128)S(1)}, f32[3,32,32]{2,1,0:T(8,128)S(1)}, u32[]{:S(2)}, u32[]{:S(2)}) collective-permute-start(f32[3,32,32]{2,1,0:T(8,128)S(1)} %fusion.39), channel_id=1, source_target_pairs={{8,0},{16,8},{24,16},{9,1},{17,9},{25,17},{10,2},{18,10},{26,18},{... | collective-permute-start | bytes 36872 | tf_op jit(solution)/shard_map/ppermute | solution.py:16
  118.2 6.6 copy-start.14
  118.3 6.6 collective-permute-start.2
  231.9 40.9 %collective-permute-start.10 = (bf16[16,400,256]{2,1,0:T(8,128)(2,1)}, bf16[16,400,256]{2,1,0:T(8,128)(2,1)}, u32[]{:S(2)}, u32[]{:S(2)}) collective-permute-start(bf16[16,400,256]{2,1,0:T(8,128)(2,1)} %get-tuple-element.39), channel_id=1, source_target_pairs={{3,7},{4,0},{11,15},{12,8},{19,23},{20,16},{27,31},{28,24}} | collective-permute-start | bytes 9830408 | tf_op jit(solution)/shard_map/ppermute | solution.py:115
  233.1 112.2 %collective-permute-start.9 = (bf16[32,400,256]{2,1,0:T(8,128)(2,1)S(1)}, bf16[32,400,256]{2,1,0:T(8,128)(2,1)S(1)}, u32[]{:S(2)}, u32[]{:S(2)}) collective-permute-start(bf16[32,400,256]{2,1,0:T(8,128)(2,1)S(1)} %get-tuple-element.32.part_ref), channel_id=1, source_target_pairs={{1,0},{2,1},{3,2},{5,4},{6,5},{7,6},{9,8},{10,9},{11,10},{13,12},{... | collective-permute-start | bytes 19660808 | tf_op jit(solution)/shard_map/ppermute | solution.py:119
  234.4 111.0 %collective-permute-start.8 = (bf16[32,400,256]{2,1,0:T(8,128)(2,1)S(1)}, bf16[32,400,256]{2,1,0:T(8,128)(2,1)S(1)}, u32[]{:S(2)}, u32[]{:S(2)}) collective-permute-start(bf16[32,400,256]{2,1,0:T(8,128)(2,1)S(1)} %get-tuple-element.32.part_ref), channel_id=1, source_target_pairs={{0,1},{1,2},{2,3},{4,5},{5,6},{6,7},{8,9},{9,10},{10,11},{12,13},{... | collective-permute-start | bytes 19660808 | tf_op jit(solution)/shard_map/ppermute | solution.py:118
  238.3 47.3 %collective-permute-start.12 = (bf16[16,400,256]{2,1,0:T(8,128)(2,1)S(1)}, bf16[16,400,256]{2,1,0:T(8,128)(2,1)S(1)}, u32[]{:S(2)}, u32[]{:S(2)}) collective-permute-start(bf16[16,400,256]{2,1,0:T(8,128)(2,1)S(1)} %get-tuple-element.38), channel_id=1, source_target_pairs={{3,4},{4,3},{11,12},{12,11},{19,20},{20,19},{27,28},{28,27}} | collective-permute-start | bytes 9830408 | tf_op jit(solution)/shard_map/ppermute | solution.py:116
  272.7 72.7 %collective-permute-start.11 = (bf16[16,400,256]{2,1,0:T(8,128)(2,1)}, bf16[16,400,256]{2,1,0:T(8,128)(2,1)}, u32[]{:S(2)}, u32[]{:S(2)}) collective-permute-start(bf16[16,400,256]{2,1,0:T(8,128)(2,1)} %collective-permute-done.10), channel_id=1, source_target_pairs={{7,4},{0,3},{15,12},{8,11},{23,20},{16,19},{31,28},{24,27}} | collective-permute-start | bytes 9830408 | tf_op jit(solution)/shard_map/ppermute | solution.py:120
  285.5 1.7 copy-start.8
  345.4 2.8 copy-start.4
  348.2 2.9 copy-start.5
  351.0 1.9 copy-start.9
  438.4 41.1 %collective-permute-start.15 = (bf16[16,400,256]{2,1,0:T(8,128)(2,1)}, bf16[16,400,256]{2,1,0:T(8,128)(2,1)}, u32[]{:S(2)}, u32[]{:S(2)}) collective-permute-start(bf16[16,400,256]{2,1,0:T(8,128)(2,1)} %get-tuple-element.37), channel_id=1, source_target_pairs={{3,7},{4,0},{11,15},{12,8},{19,23},{20,16},{27,31},{28,24}} | collective-permute-start | bytes 9830408 | tf_op jit(solution)/shard_map/ppermute | solution.py:115
  439.7 112.7 %collective-permute-start.14 = (bf16[32,400,256]{2,1,0:T(8,128)(2,1)S(1)}, bf16[32,400,256]{2,1,0:T(8,128)(2,1)S(1)}, u32[]{:S(2)}, u32[]{:S(2)}) collective-permute-start(bf16[32,400,256]{2,1,0:T(8,128)(2,1)S(1)} %get-tuple-element.30.part_ref), channel_id=1, source_target_pairs={{1,0},{2,1},{3,2},{5,4},{6,5},{7,6},{9,8},{10,9},{11,10},{13,12},{... | collective-permute-start | bytes 19660808 | tf_op jit(solution)/shard_map/ppermute | solution.py:119
  441.0 111.4 %collective-permute-start.13 = (bf16[32,400,256]{2,1,0:T(8,128)(2,1)S(1)}, bf16[32,400,256]{2,1,0:T(8,128)(2,1)S(1)}, u32[]{:S(2)}, u32[]{:S(2)}) collective-permute-start(bf16[32,400,256]{2,1,0:T(8,128)(2,1)S(1)} %get-tuple-element.30.part_ref), channel_id=1, source_target_pairs={{0,1},{1,2},{2,3},{4,5},{5,6},{6,7},{8,9},{9,10},{10,11},{12,13},{... | collective-permute-start | bytes 19660808 | tf_op jit(solution)/shard_map/ppermute | solution.py:118
  445.4 47.0 %collective-permute-start.17 = (bf16[16,400,256]{2,1,0:T(8,128)(2,1)S(1)}, bf16[16,400,256]{2,1,0:T(8,128)(2,1)S(1)}, u32[]{:S(2)}, u32[]{:S(2)}) collective-permute-start(bf16[16,400,256]{2,1,0:T(8,128)(2,1)S(1)} %get-tuple-element.36), channel_id=1, source_target_pairs={{3,4},{4,3},{11,12},{12,11},{19,20},{20,19},{27,28},{28,27}} | collective-permute-start | bytes 9830408 | tf_op jit(solution)/shard_map/ppermute | solution.py:116
  479.5 73.0 %collective-permute-start.16 = (bf16[16,400,256]{2,1,0:T(8,128)(2,1)}, bf16[16,400,256]{2,1,0:T(8,128)(2,1)}, u32[]{:S(2)}, u32[]{:S(2)}) collective-permute-start(bf16[16,400,256]{2,1,0:T(8,128)(2,1)} %collective-permute-done.15), channel_id=1, source_target_pairs={{7,4},{0,3},{15,12},{8,11},{23,20},{16,19},{31,28},{24,27}} | collective-permute-start | bytes 9830408 | tf_op jit(solution)/shard_map/ppermute | solution.py:120
  492.4 1.7 copy-start.10
  552.4 2.8 copy-start.6
  555.2 2.9 copy-start.7
  558.1 1.9 copy-start.11
  649.6 41.3 %collective-permute-start.20 = (bf16[16,400,256]{2,1,0:T(8,128)(2,1)S(1)}, bf16[16,400,256]{2,1,0:T(8,128)(2,1)}, u32[]{:S(2)}, u32[]{:S(2)}) collective-permute-start(bf16[16,400,256]{2,1,0:T(8,128)(2,1)S(1)} %get-tuple-element.35), channel_id=1, source_target_pairs={{3,7},{4,0},{11,15},{12,8},{19,23},{20,16},{27,31},{28,24}} | collective-permute-start | bytes 9830408 | tf_op jit(solution)/shard_map/ppermute | solution.py:115
  650.9 112.9 %collective-permute-start.19 = (bf16[32,400,256]{2,1,0:T(8,128)(2,1)}, bf16[32,400,256]{2,1,0:T(8,128)(2,1)}, u32[]{:S(2)}, u32[]{:S(2)}) collective-permute-start(bf16[32,400,256]{2,1,0:T(8,128)(2,1)} %get-tuple-element.28.part_ref), channel_id=1, source_target_pairs={{1,0},{2,1},{3,2},{5,4},{6,5},{7,6},{9,8},{10,9},{11,10},{13,12},{... | collective-permute-start | bytes 19660808 | tf_op jit(solution)/shard_map/ppermute | solution.py:119
  652.2 111.6 %collective-permute-start.18 = (bf16[32,400,256]{2,1,0:T(8,128)(2,1)}, bf16[32,400,256]{2,1,0:T(8,128)(2,1)}, u32[]{:S(2)}, u32[]{:S(2)}) collective-permute-start(bf16[32,400,256]{2,1,0:T(8,128)(2,1)} %get-tuple-element.28.part_ref), channel_id=1, source_target_pairs={{0,1},{1,2},{2,3},{4,5},{5,6},{6,7},{8,9},{9,10},{10,11},{12,13},{... | collective-permute-start | bytes 19660808 | tf_op jit(solution)/shard_map/ppermute | solution.py:118
  658.8 49.1 %collective-permute-start.22 = (bf16[16,400,256]{2,1,0:T(8,128)(2,1)}, bf16[16,400,256]{2,1,0:T(8,128)(2,1)}, u32[]{:S(2)}, u32[]{:S(2)}) collective-permute-start(bf16[16,400,256]{2,1,0:T(8,128)(2,1)} %get-tuple-element.34), channel_id=1, source_target_pairs={{3,4},{4,3},{11,12},{12,11},{19,20},{20,19},{27,28},{28,27}} | collective-permute-start | bytes 9830408 | tf_op jit(solution)/shard_map/ppermute | solution.py:116
  690.9 72.9 %collective-permute-start.21 = (bf16[16,400,256]{2,1,0:T(8,128)(2,1)}, bf16[16,400,256]{2,1,0:T(8,128)(2,1)}, u32[]{:S(2)}, u32[]{:S(2)}) collective-permute-start(bf16[16,400,256]{2,1,0:T(8,128)(2,1)} %collective-permute-done.20), channel_id=1, source_target_pairs={{7,4},{0,3},{15,12},{8,11},{23,20},{16,19},{31,28},{24,27}} | collective-permute-start | bytes 9830408 | tf_op jit(solution)/shard_map/ppermute | solution.py:120
  865.3 10.7 %copy-start.1 = (f32[1,32,20,32]{3,1,2,0:T(8,128)S(1)}, f32[1,32,20,32]{3,1,2,0:T(8,128)}, u32[]{:S(2)}) copy-start(f32[1,32,20,32]{3,1,2,0:T(8,128)} %param.10) | copy-start | bytes 245764
